TPU v7x, 32 devices: a whole 2x2x4 slice. The times are simulated.
32 devices in a mesh: groups: 2 (over x), seq: 4 (over y, core), tp: 4 (over z).
Axes of the slice: x: 2, y: 2, z: 4, core: 2. Of those that a mesh axis runs over, the one named last changes fastest.
Arguments:
- hidden: bfloat16 [768, 16384], P(('groups', 'tp'), 'seq'), parts along dimension 0, may hold values from -7 to 7
- w_query: bfloat16 [16384, 16384], P('seq', 'tp'), may hold values from -0.1875 to 0.1875
- w_key: bfloat16 [16384, 1024], P('seq', 'tp'), may hold values from -0.046875 to 0.046875
- w_value: bfloat16 [16384, 1024], P('seq', 'tp'), may hold values from -0.046875 to 0.046875
- w_out: bfloat16 [16384, 16384], P('tp', 'seq'), may hold values from -0.046875 to 0.046875
- vert_blocks: int32 [256, 3], P(('groups', 'tp')), parts along dimension 0, may hold values from 0 to 2, as said below
- vert_count: int32 [256], P(('groups', 'tp')), parts along dimension 0, may hold values from 1 to 3, as said below
- slash_offsets: int32 [256, 3], P(('groups', 'tp')), parts along dimension 0, may hold values from 0 to 2, as said below
- slash_count: int32 [256], P(('groups', 'tp')), parts along dimension 0, may hold values from 1 to 3, as said below
Outputs:
- attn_out: bfloat16 [768, 16384], P(('groups', 'tp'), 'seq'), parts along dimension 0
There are 2 independent parts, one for each index of `groups`. A program takes and returns all parts, laid end to end along the dimension named above; an argument that names none is the same for every part. Nothing has to cross between parts.
Inputs may be any that keep to these rules, and one draw needn't show every extreme that they name: `vert_blocks`: each head's 3 entries are distinct block indices; only the first vert_count of them are used. `vert_count`: some head has exactly 3. `slash_offsets`: each head's 3 entries are distinct and the first is 0; only the first slash_count of them are used. `slash_count`: some head has exactly 3.
All inputs are finite; a program needn't handle non-finite values.
Results may differ from a plain program's by a relative error of at most 0.012.
The roundings to bfloat16 on the way count: a program that leaves them out, or rounds other values in their place, can miss the bound.
Values may be sent and summed in bfloat16 or wider, within the bound.
A program may use at most 192 MiB of HBM per device.

v0:
```python
import math

import jax
import jax.numpy as jnp
from jax import lax
from jax.sharding import PartitionSpec as P

HEAD_DIM = 128
BLOCK = 128
VERT = 3
SLASH = 3


NEG_FILL = -1e30


def rope_tables(positions):
    pair_index = jnp.arange(HEAD_DIM // 2, dtype=jnp.float32)
    base_freq = jnp.exp(-(2.0 * pair_index / HEAD_DIM) * jnp.log(500000.0))
    wavelength = 2.0 * jnp.pi / base_freq
    smooth = (8192.0 / wavelength - 1.0) / 3.0
    blended = (1.0 - smooth) * base_freq / 8.0 + smooth * base_freq
    scaled = jnp.where(
        wavelength < 2048.0, base_freq, jnp.where(wavelength > 8192.0, base_freq / 8.0, blended)
    )
    angles = positions.astype(jnp.float32)[:, None] * scaled[None, :]
    return (jnp.cos(angles), jnp.sin(angles))


def rotate_pairs(values, cos_table, sin_table):
    paired = values.reshape(values.shape[:-1] + (HEAD_DIM // 2, 2))
    real_part = paired[..., 0]
    imag_part = paired[..., 1]
    turned = jnp.stack(
        [
            real_part * cos_table - imag_part * sin_table,
            real_part * sin_table + imag_part * cos_table,
        ],
        axis=-1,
    )
    return turned.reshape(values.shape)


def attend(
    query_heads,
    key_all,
    value_all,
    vert_list,
    vert_live,
    slash_list,
    slash_live,
    vert_bound,
    slash_bound,
):
    heads_here = query_heads.shape[0]
    tokens = query_heads.shape[1]
    blocks = tokens // BLOCK
    score_scale = 1.0 / math.sqrt(HEAD_DIM)
    query_blocks = query_heads.reshape(heads_here, blocks, BLOCK, HEAD_DIM)
    key_blocks = key_all.reshape(blocks, BLOCK, HEAD_DIM)
    value_blocks = value_all.reshape(blocks, BLOCK, HEAD_DIM)
    block_ids = jnp.arange(blocks, dtype=jnp.int32)
    within = jnp.arange(BLOCK, dtype=jnp.int32)
    causal = (within[None, :] <= within[:, None])[None, None]
    vert_in_use = jnp.arange(VERT, dtype=jnp.int32)[None, :] < vert_live[:, None]
    slash_in_use = jnp.arange(SLASH, dtype=jnp.int32)[None, :] < slash_live[:, None]
    vert_member = jnp.any(
        (vert_list[:, :, None] == block_ids[None, None, :]) & vert_in_use[:, :, None], axis=1
    )

    def vertical_slot(slot_id):
        column = lax.dynamic_index_in_dim(vert_list, slot_id, 1, keepdims=False)
        in_use = lax.dynamic_index_in_dim(vert_in_use, slot_id, 1, keepdims=False)
        chosen_keys = key_blocks[column]
        scores = (
            jnp.einsum(
                "hnqd,hkd->hnqk", query_blocks, chosen_keys, preferred_element_type=jnp.float32
            )
            * score_scale
        )
        earlier = (column[:, None] < block_ids[None, :])[:, :, None, None]
        same_block = (column[:, None] == block_ids[None, :])[:, :, None, None]
        visible = in_use[:, None, None, None] & (earlier | same_block & causal)
        return (scores, visible, value_blocks[column])

    def slash_slot(slot_id):
        offset = lax.dynamic_index_in_dim(slash_list, slot_id, 1, keepdims=False)
        in_use = lax.dynamic_index_in_dim(slash_in_use, slot_id, 1, keepdims=False)
        target = block_ids[None, :] - offset[:, None]
        safe_target = jnp.maximum(target, 0)
        covered = jnp.take_along_axis(vert_member, safe_target, axis=1)
        chosen_keys = key_blocks[safe_target]
        scores = (
            jnp.einsum(
                "hnqd,hnkd->hnqk", query_blocks, chosen_keys, preferred_element_type=jnp.float32
            )
            * score_scale
        )
        reach = ((target >= 0) & jnp.logical_not(covered))[:, :, None, None]
        diagonal = (offset == 0)[:, None, None, None]
        visible = in_use[:, None, None, None] & reach & (jnp.logical_not(diagonal) | causal)
        return (scores, visible, value_blocks[safe_target])

    def gather_stats(slot_fn):

        def gather_update(slot_id, running):
            row_max, row_sum = running
            scores, visible, unused_values = slot_fn(slot_id)
            masked = jnp.where(visible, scores, NEG_FILL)
            fresh_max = jnp.maximum(row_max, jnp.max(masked, axis=-1, keepdims=True))
            kept_terms = jnp.where(visible, jnp.exp(masked - fresh_max), 0.0)
            return (
                fresh_max,
                row_sum * jnp.exp(row_max - fresh_max)
                + jnp.sum(kept_terms, axis=-1, keepdims=True),
            )

        return gather_update

    stats_shape = (heads_here, blocks, BLOCK, 1)
    running = (jnp.full(stats_shape, NEG_FILL, jnp.float32), jnp.zeros(stats_shape, jnp.float32))
    running = lax.fori_loop(0, vert_bound, gather_stats(vertical_slot), running)
    row_max, row_sum = lax.fori_loop(0, slash_bound, gather_stats(slash_slot), running)

    def accumulate(slot_fn, pattern):

        def accumulate_update(slot_id, totals):
            scores, visible, chosen_values = slot_fn(slot_id)
            weights = jnp.where(
                visible, jnp.exp(jnp.where(visible, scores, NEG_FILL) - row_max), 0.0
            )
            weights_low = (weights / row_sum).astype(jnp.bfloat16)
            return totals + jnp.einsum(
                pattern, weights_low, chosen_values, preferred_element_type=jnp.float32
            )

        return accumulate_update

    totals = jnp.zeros((heads_here, blocks, BLOCK, HEAD_DIM), jnp.float32)
    totals = lax.fori_loop(0, vert_bound, accumulate(vertical_slot, "hnqk,hkd->hnqd"), totals)
    totals = lax.fori_loop(0, slash_bound, accumulate(slash_slot, "hnqk,hnkd->hnqd"), totals)
    return totals.astype(jnp.bfloat16).reshape(heads_here, tokens, HEAD_DIM)


def on_device(
    hidden, w_query, w_key, w_value, w_out, vert_blocks, vert_count, slash_offsets, slash_count
):
    seq_size = lax.axis_size("seq")
    seq_rank = lax.axis_index("seq")
    width_query = w_query.shape[1]
    width_pair = w_key.shape[1]
    group_heads = width_query // HEAD_DIM
    group_pairs = width_pair // HEAD_DIM
    heads_here = group_heads // seq_size
    segment = lax.all_gather(hidden, "tp", axis=0, tiled=True)
    projected = jnp.concatenate(
        [
            jnp.dot(segment, w_query, preferred_element_type=jnp.float32),
            jnp.dot(segment, w_key, preferred_element_type=jnp.float32),
            jnp.dot(segment, w_value, preferred_element_type=jnp.float32),
        ],
        axis=1,
    )
    tokens = projected.shape[0]
    query_term = projected[:, :width_query]
    pair_term = projected[:, width_query:]
    query_rows, pair_rows = (
        lax.psum_scatter(query_term, "seq", scatter_dimension=0, tiled=True),
        lax.psum_scatter(pair_term, "seq", scatter_dimension=0, tiled=True),
    )
    rows_here = query_rows.shape[0]
    cos_table, sin_table = rope_tables(
        seq_rank * rows_here + jnp.arange(rows_here, dtype=jnp.int32)
    )
    query_rows = rotate_pairs(
        query_rows.reshape(rows_here, group_heads, HEAD_DIM),
        cos_table[:, None, :],
        sin_table[:, None, :],
    )
    query_rows = query_rows.astype(jnp.bfloat16).reshape(rows_here, width_query)
    key_rows = rotate_pairs(
        pair_rows[:, :width_pair].reshape(rows_here, group_pairs, HEAD_DIM),
        cos_table[:, None, :],
        sin_table[:, None, :],
    )
    key_rows = key_rows.astype(jnp.bfloat16)
    value_rows = (
        pair_rows[:, width_pair:].astype(jnp.bfloat16).reshape(rows_here, group_pairs, HEAD_DIM)
    )
    both_rows = jnp.concatenate([key_rows, value_rows], axis=2)
    spread = jnp.repeat(both_rows, seq_size // group_pairs, axis=1).reshape(
        rows_here, seq_size * 2 * HEAD_DIM
    )
    query_local, pair_local = (
        lax.all_to_all(query_rows, "seq", split_axis=1, concat_axis=0, tiled=True),
        lax.all_to_all(spread, "seq", split_axis=1, concat_axis=0, tiled=True),
    )
    key_all = pair_local[:, :HEAD_DIM]
    value_all = pair_local[:, HEAD_DIM:]
    first_head = seq_rank * heads_here
    vert_list = lax.dynamic_slice_in_dim(vert_blocks, first_head, heads_here, 0)
    vert_live = lax.dynamic_slice_in_dim(vert_count, first_head, heads_here, 0)
    slash_list = lax.dynamic_slice_in_dim(slash_offsets, first_head, heads_here, 0)
    slash_live = lax.dynamic_slice_in_dim(slash_count, first_head, heads_here, 0)
    vert_bound = VERT
    slash_bound = SLASH
    query_heads = query_local.reshape(tokens, heads_here, HEAD_DIM).transpose(1, 0, 2)
    attended = attend(
        query_heads,
        key_all,
        value_all,
        vert_list,
        vert_live,
        slash_list,
        slash_live,
        vert_bound,
        slash_bound,
    )
    head_local = attended.transpose(1, 0, 2).reshape(tokens, heads_here * HEAD_DIM)
    gathered = lax.all_gather(head_local, "seq", axis=1, tiled=True)
    summed = lax.psum_scatter(
        jnp.dot(gathered, w_out, preferred_element_type=jnp.float32).astype(jnp.bfloat16),
        "tp",
        scatter_dimension=0,
        tiled=True,
    )
    return summed


def solution(mesh):
    in_specs = (
        P(("groups", "tp"), "seq"),
        P("seq", "tp"),
        P("seq", "tp"),
        P("seq", "tp"),
        P("tp", "seq"),
        P(("groups", "tp"), None),
        P(("groups", "tp")),
        P(("groups", "tp"), None),
        P(("groups", "tp")),
    )
    out_specs = P(("groups", "tp"), "seq")
    return jax.shard_map(
        on_device, mesh=mesh, in_specs=in_specs, out_specs=out_specs, check_vma=False
    )
```

profile of v0, /device:TPU:0, one launch (start us, length us, event | category | flops | bytes accessed | tf_op | source)
XLA Modules:
  0.0 360.1 jit_solution(5187170436590478264)
XLA Ops:
  6.5 0.7 all-gather.3.cloned.1.call-update
  7.3 67.9 %all-gather.3.cloned.1.call-done = bf16[384,4096]{1,0:T(8,128)(2,1)} async-done(((bf16[96,4096]{1,0:T(8,128)(2,1)}), bf16[384,4096]{1,0:T(8,128)(2,1)}) %all-gather.3.cloned.1.call-update) | async-done | bytes 3145744 | tf_op jit(solution)/shard_map/all_gather | solution.py:155
  75.2 3.3 fusion.85
  78.7 1.3 fusion.86
  80.0 1.1 copy.84
  81.2 22.1 %fusion.87 = f32[384,4096]{1,0:T(8,128)} fusion(bf16[384,4096]{1,0:T(8,128)(2,1)} %all-gather.3.cloned.1.call-done, bf16[4096,4096]{1,0:T(8,128)(2,1)} %param.20), kind=kOutput, calls=%fused_computation.152 | convolution fusion | flops 12884901888 | bytes 42991616 | tf_op jit(solution)/shard_map/dot_general | solution.py:158
  104.3 0.9 slice.49
  105.3 0.9 slice.52
  106.8 0.7 broadcast_in_dim.184
  107.6 3.4 all-to-all-start
  110.9 53.4 %reduce-scatter.6.cloned.1.call-done = f32[96,4096]{1,0:T(8,128)} async-done(((f32[384,4096]{1,0:T(8,128)}), f32[96,4096]{1,0:T(8,128)}) %reduce-scatter.6.cloned.1.call-update) | async-done | bytes 1572880 | tf_op jit(solution)/shard_map/reduce_scatter | solution.py:168
  164.4 1.8 copy.72
  166.2 2.9 subtract_convert_fusion
  169.1 2.8 pad_maximum_fusion
  171.9 1.2 copy.73
  173.2 3.7 %all-to-all-start.1 = ((bf16[96,4,1024]{2,0,1:T(8,128)(2,1)}), bf16[96,4,1024]{2,0,1:T(8,128)(2,1)S(1)}, u32[]{:S(2)}, u32[]{:S(2)}) async-start(bf16[96,4,1024]{2,0,1:T(8,128)(2,1)} %copy.73), calls=%async_computation.2 | async-start | bytes 1572864 | tf_op jit(solution)/shard_map/all_to_all | solution.py:195
  177.2 11.3 %all-to-all-done.1 = bf16[96,4,1024]{2,0,1:T(8,128)(2,1)S(1)} async-done(((bf16[96,4,1024]{2,0,1:T(8,128)(2,1)}), bf16[96,4,1024]{2,0,1:T(8,128)(2,1)S(1)}, u32[]{:S(2)}, u32[]{:S(2)}) %all-to-all-start.1) | async-done | bytes 786464 | tf_op jit(solution)/shard_map/all_to_all | solution.py:195
  188.8 6.3 %while.66 = (s32[]{:T(128)}, f32[8,3,128,1]{2,1,0,3:T(4,128)S(1)}, f32[8,3,128,1]{2,1,0,3:T(4,128)S(1)}, pred[8,3]{0,1:T(4,128)(4,1)S(1)}, s32[8,3]{0,1:T(4,128)...) while((s32[]{:T(128)}, f32[8,3,128,1]{2,1,0,3:T(4,128)S(1)}, ...), condition=%wide.region_5.6_spmd.clone.clone, body=%wide.region_2.5_spmd.clone.clone.sunk | while | flops 105414728 | bytes 4932064 | solution.py:122
  190.2 0.7 select_reduce_fusion.2
  195.2 10.9 %while.64 = (s32[]{:T(128)}, f32[8,3,128,1]{2,1,0,3:T(4,128)S(1)}, f32[8,3,128,1]{2,1,0,3:T(4,128)S(1)}, pred[8,3]{0,1:T(4,128)(4,1)S(1)}, s32[8,3]{0,1:T(4,128)...) while((s32[]{:T(128)}, f32[8,3,128,1]{2,1,0,3:T(4,128)S(1)}, ...), condition=%wide.region_10.12_spmd.clone.clone, body=%wide.region_7.11_spmd.clone.clone.sunk | while | flops 103964072 | bytes 6883309 | solution.py:123
  195.5 0.8 gather_fusion.1
  196.7 0.7 gather_fusion
  199.2 0.8 gather_fusion.1
  200.4 0.7 gather_fusion
  202.8 0.8 gather_fusion.1
  204.0 0.7 gather_fusion
  206.1 13.6 %while.67 = (s32[]{:T(128)}, f32[8,3,128,128]{3,2,1,0:T(8,128)}, pred[8,3]{0,1:T(4,128)(4,1)S(1)}, s32[8,3]{0,1:T(4,128)S(1)}, bf16[3,128,128]{2,1,0:T(8,128)(2,...) while((s32[]{:T(128)}, f32[8,3,128,128]{3,2,1,0:T(8,128)}, ...), condition=%wide.region_12.14_spmd.clone.clone, body=%wide.region_11.13_spmd.clone.clone.sunk | while | flops 205669456 | bytes 5566935 | solution.py:140
  207.5 2.3 select_add_fusion.2
  211.1 3.7 %select_add_fusion.2 = f32[8,3,128,128]{3,2,1,0:T(8,128)} fusion(f32[8,3,128,128]{3,2,1,0:T(8,128)} %get-tuple-element.1472, bf16[8,3,128,128]{3,2,1,0:T(8,128)(2,1)S(1)} %get-tuple-element.1487, f32[8,3,128]{2,1,0:T(4,128)S(1)} %bitcast.229, f32[8,3,128]{2,1,0:T(4,128)S(1)} %bitcast.222, pred[8]{0:T(512)(128)(4,1)S(1)} %dynamic-slice_bitcast_fusion.15, ...), kind=kOutput, calls=%fused_computation.38.clone.1 | convolution fusion | flops 205651968 | bytes 4497465 | tf_op jit(solution)/shard_map/while/body/eval_jaxpr/hnqk,hkd->hnqd/dot_general | solution.py:133
  216.1 3.7 %select_add_fusion.2 = f32[8,3,128,128]{3,2,1,0:T(8,128)} fusion(f32[8,3,128,128]{3,2,1,0:T(8,128)} %get-tuple-element.1472, bf16[8,3,128,128]{3,2,1,0:T(8,128)(2,1)S(1)} %get-tuple-element.1487, f32[8,3,128]{2,1,0:T(4,128)S(1)} %bitcast.229, f32[8,3,128]{2,1,0:T(4,128)S(1)} %bitcast.222, pred[8]{0:T(512)(128)(4,1)S(1)} %dynamic-slice_bitcast_fusion.15, ...), kind=kOutput, calls=%fused_computation.38.clone.1 | convolution fusion | flops 205651968 | bytes 4497465 | tf_op jit(solution)/shard_map/while/body/eval_jaxpr/hnqk,hkd->hnqd/dot_general | solution.py:133
  219.7 20.4 %while.65 = (s32[]{:T(128)}, f32[8,3,128,128]{3,2,1,0:T(8,128)}, pred[8,3]{0,1:T(4,128)(4,1)S(1)}, s32[8,3]{0,1:T(4,128)S(1)}, pred[8,3]{0,1:T(4,128)(4,1)S(1)},...) while((s32[]{:T(128)}, f32[8,3,128,128]{3,2,1,0:T(8,128)}, ...), condition=%wide.region_14.16_spmd.clone.clone, body=%wide.region_13.15_spmd.clone.clone.sunk | while | flops 204621232 | bytes 8976453 | solution.py:141
  220.1 0.8 gather_fusion.4
  221.3 0.7 gather_fusion.2
  222.0 0.7 gather_fusion.3
  222.8 3.7 %convolution_add_fusion.2 = f32[8,3,128,128]{3,2,1,0:T(8,128)} fusion(f32[8,3,128,128]{3,2,1,0:T(8,128)} %get-tuple-element.1505, bf16[8,3,128,128]{3,2,1,0:T(8,128)(2,1)S(1)} %bitcast.216, bf16[8,3,128,128]{3,2,1,0:T(8,128)(2,1)S(1)} %bitcast.217, bf16[8,3,128,128]{3,2,1,0:T(8,128)(2,1)S(1)} %get-tuple-element.1521, ...), kind=kOutput, calls=%fused_computation.95.clone.1 | convolution fusion | flops 204472320 | bytes 5660696 | tf_op jit(solution)/shard_map/while/body/eval_jaxpr/hnqk,hnkd->hnqd/dot_general | solution.py:133
  226.9 0.8 gather_fusion.4
  228.1 0.7 gather_fusion.2
  228.8 0.7 gather_fusion.3
  229.6 3.7 %convolution_add_fusion.2 = f32[8,3,128,128]{3,2,1,0:T(8,128)} fusion(f32[8,3,128,128]{3,2,1,0:T(8,128)} %get-tuple-element.1505, bf16[8,3,128,128]{3,2,1,0:T(8,128)(2,1)S(1)} %bitcast.216, bf16[8,3,128,128]{3,2,1,0:T(8,128)(2,1)S(1)} %bitcast.217, bf16[8,3,128,128]{3,2,1,0:T(8,128)(2,1)S(1)} %get-tuple-element.1521, ...), kind=kOutput, calls=%fused_computation.95.clone.1 | convolution fusion | flops 204472320 | bytes 5660696 | tf_op jit(solution)/shard_map/while/body/eval_jaxpr/hnqk,hnkd->hnqd/dot_general | solution.py:133
  233.7 0.8 gather_fusion.4
  234.9 0.7 gather_fusion.2
  235.6 0.7 gather_fusion.3
  236.4 3.7 %convolution_add_fusion.2 = f32[8,3,128,128]{3,2,1,0:T(8,128)} fusion(f32[8,3,128,128]{3,2,1,0:T(8,128)} %get-tuple-element.1505, bf16[8,3,128,128]{3,2,1,0:T(8,128)(2,1)S(1)} %bitcast.216, bf16[8,3,128,128]{3,2,1,0:T(8,128)(2,1)S(1)} %bitcast.217, bf16[8,3,128,128]{3,2,1,0:T(8,128)(2,1)S(1)} %get-tuple-element.1521, ...), kind=kOutput, calls=%fused_computation.95.clone.1 | convolution fusion | flops 204472320 | bytes 5660696 | tf_op jit(solution)/shard_map/while/body/eval_jaxpr/hnqk,hnkd->hnqd/dot_general | solution.py:133
  240.1 1.5 convert_element_type.41
  241.7 1.2 copy.78
  243.1 28.4 %all-gather.5.cloned.1.call-done = bf16[384,4096]{0,1:T(8,128)(2,1)} async-done(((bf16[384,1024]{0,1:T(8,128)(2,1)}), bf16[384,4096]{0,1:T(8,128)(2,1)}) %all-gather.5.cloned.1.call-update) | async-done | bytes 3145744 | tf_op jit(solution)/shard_map/all_gather | solution.py:220
  271.6 21.5 %convolution_convert_fusion = bf16[384,4096]{1,0:T(8,128)(2,1)} fusion(bf16[384,4096]{0,1:T(8,128)(2,1)} %all-gather.5.cloned.1.call-done, bf16[4096,4096]{1,0:T(8,128)(2,1)} %param.23), kind=kOutput, calls=%fused_computation.126 | convolution fusion | flops 12886474752 | bytes 39845888 | tf_op jit(solution)/shard_map/dot_general | solution.py:222
  293.1 60.4 %reduce-scatter.8.cloned.1.call-done = bf16[96,4096]{1,0:T(8,128)(2,1)} async-done(((bf16[384,4096]{1,0:T(8,128)(2,1)}), bf16[96,4096]{1,0:T(8,128)(2,1)}) %reduce-scatter.8.cloned.1.call-update) | async-done | bytes 786448 | tf_op jit(solution)/shard_map/reduce_scatter | solution.py:221
  (201 shorter events, 20.7 us)
Async XLA Ops:
  6.5 68.6 %copy-start = (bf16[4096,256]{1,0:T(8,128)(2,1)S(1)}, bf16[4096,256]{1,0:T(8,128)(2,1)}, u32[]{:S(2)}) copy-start(bf16[4096,256]{1,0:T(8,128)(2,1)} %param.21) | copy-start | bytes 6291460
  6.5 68.6 %all-gather.3.cloned.1.call-start = ((), (), s32[]{:S(2)}) async-start(), calls=%async_computation.5 | async-start | bytes 3932160 | tf_op jit(solution)/shard_map/all_gather | solution.py:155
  7.3 97.0 %reduce-scatter.10.cloned.1.call-start = ((), (), s32[]{:S(2)}) async-start(), calls=%async_computation.9 | async-start | bytes 983040
  75.2 3.3 copy-start.4
  75.2 3.5 copy-start.5
  81.2 83.2 %reduce-scatter.6.cloned.1.call-start = ((), (), s32[]{:S(2)}) async-start(), calls=%async_computation.6 | async-start | bytes 7864320 | tf_op jit(solution)/shard_map/reduce_scatter | solution.py:168
  103.3 0.7 copy-start.6
  107.6 65.6 %all-to-all-start = ((bf16[96,4,256]{2,0,1:T(8,128)(2,1)}), bf16[96,4,256]{2,0,1:T(8,128)(2,1)S(1)}, u32[]{:S(2)}, u32[]{:S(2)}) async-start(bf16[96,4,256]{2,0,1:T(8,128)(2,1)} %bitcast.3), calls=%async_computation | async-start | bytes 393216 | tf_op jit(solution)/shard_map/all_to_all | solution.py:196
  171.9 5.0 %copy-start.2 = (s32[32,3]{0,1:T(4,128)S(1)}, s32[32,3]{0,1:T(4,128)}, u32[]{:S(2)}) copy-start(s32[32,3]{0,1:T(4,128)} %param.26) | copy-start | bytes 1156
  171.9 5.0 %copy-start.3 = (s32[32,3]{0,1:T(4,128)S(1)}, s32[32,3]{0,1:T(4,128)}, u32[]{:S(2)}) copy-start(s32[32,3]{0,1:T(4,128)} %param.24) | copy-start | bytes 1156
  171.9 5.1 %copy-start.7 = (s32[32]{0:T(128)S(1)}, s32[32]{0:T(128)}, u32[]{:S(2)}) copy-start(s32[32]{0:T(128)} %param.27) | copy-start | bytes 388
  173.2 15.3 %all-to-all-start.1 = ((bf16[96,4,1024]{2,0,1:T(8,128)(2,1)}), bf16[96,4,1024]{2,0,1:T(8,128)(2,1)S(1)}, u32[]{:S(2)}, u32[]{:S(2)}) async-start(bf16[96,4,1024]{2,0,1:T(8,128)(2,1)} %copy.73), calls=%async_computation.2 | async-start | bytes 1572864 | tf_op jit(solution)/shard_map/all_to_all | solution.py:195
  176.9 94.7 %all-gather.5.cloned.1.call-start = ((), (), s32[]{:S(2)}) async-start(), calls=%async_computation.7 | async-start | bytes 3932160 | tf_op jit(solution)/shard_map/all_gather | solution.py:220
  242.9 110.7 %reduce-scatter.8.cloned.1.call-start = ((), (), s32[]{:S(2)}) async-start(), calls=%async_computation.8 | async-start | bytes 3932160 | tf_op jit(solution)/shard_map/reduce_scatter | solution.py:221
  293.1 60.4 %copy-start.1 = (bf16[4096,256]{1,0:T(8,128)(2,1)S(1)}, bf16[4096,256]{1,0:T(8,128)(2,1)}, u32[]{:S(2)}) copy-start(bf16[4096,256]{1,0:T(8,128)(2,1)} %param.21) | copy-start | bytes 6291460
Sparse Core Ops, SparseCore 0:
  8.9 66.1 all-gather.2
  81.3 21.8 reduce-scatter.9
  105.9 58.3 reduce-scatter.5
  243.0 28.5 all-gather.4
  293.2 60.2 reduce-scatter.7
where the time goes:
time: 361 us; the launch traced here: 360 us
  waiting for transfers between devices  222 us (61%)
  matrix products  72.7 us (20%)
  local copies, waits for them, and re-layouts  28.9 us (8%)
  other arithmetic  14.6 us (4%)
  between operations  13.4 us (4%)
  starting transfers between devices  7.43 us (2%)
    all_gather x1, waiting for transfers between devices, on_device(): segment = lax.all_gather(hidden, 'tp', axis=0, tiled=True)  67.9 us
    reduce_scatter x1, waiting for transfers between devices, on_device(): lax.psum_scatter(jnp.dot(gathered, w_out, preferred_element_type=jnp.floa...  60.4 us
    reduce_scatter x1, waiting for transfers between devices, on_device(): lax.psum_scatter(query_term, 'seq', scatter_dimension=0, tiled=True)  53.4 us
    all_gather x1, waiting for transfers between devices, on_device(): gathered = lax.all_gather(head_local, 'seq', axis=1, tiled=True)  28.4 us
    dot_general x1, matrix products, on_device(): jnp.dot(segment, w_query, preferred_element_type=jnp.float32)  22.1 us
    dot_general x1, matrix products, on_device(): jnp.dot(gathered, w_out, preferred_element_type=jnp.float32)  21.5 us
    dot_general x6, matrix products, accumulate_update(): jnp.einsum(pattern, weights_low, chosen_values, preferred_element_type=jn...  20.7 us
    all_to_all x1, waiting for transfers between devices, on_device(): lax.all_to_all(query_rows, 'seq', split_axis=1, concat_axis=0, tiled=True)  11.3 us
  transfers between devices with their start and end apart: 7, of which 5 were waited for; matrix products, arithmetic and copies ran while one was open for 10% of the time, Pallas kernels for 0%

commit v1 on v0

v1 whole, which is shorter than its diff:
```python
import functools
import math

import jax
import jax.numpy as jnp
from jax import lax
from jax.experimental import pallas as pl
from jax.experimental.pallas import tpu as pltpu
from jax.sharding import PartitionSpec as P

HEAD_DIM = 128
BLOCK = 128
VERT = 3
SLASH = 3


NEG_FILL = -1e30


def rope_tables(positions):
    pair_index = jnp.arange(HEAD_DIM // 2, dtype=jnp.float32)
    base_freq = jnp.exp(-(2.0 * pair_index / HEAD_DIM) * jnp.log(500000.0))
    wavelength = 2.0 * jnp.pi / base_freq
    smooth = (8192.0 / wavelength - 1.0) / 3.0
    blended = (1.0 - smooth) * base_freq / 8.0 + smooth * base_freq
    scaled = jnp.where(
        wavelength < 2048.0, base_freq, jnp.where(wavelength > 8192.0, base_freq / 8.0, blended)
    )
    angles = positions.astype(jnp.float32)[:, None] * scaled[None, :]
    return (jnp.cos(angles), jnp.sin(angles))


def attend_kernel(
    heads_here,
    query_ref,
    pair_ref,
    cos_ref,
    sin_ref,
    vert_ref,
    vert_live_ref,
    slash_ref,
    slash_live_ref,
    out_ref,
    key_ref,
    value_ref,
):
    tokens = query_ref.shape[0]
    blocks = tokens // BLOCK
    score_scale = 1.0 / math.sqrt(HEAD_DIM)
    even = lax.broadcasted_iota(jnp.int32, (tokens, HEAD_DIM), 1) % 2 == 0

    def rotate(raw):
        swapped = jnp.where(
            even, pltpu.roll(raw, HEAD_DIM - 1, 1), pltpu.roll(raw, 1, 1)
        )
        return (raw * cos_ref[...] + swapped * sin_ref[...]).astype(jnp.bfloat16)

    @pl.when(pl.program_id(0) == 0)
    def _():
        key_ref[...] = rotate(pair_ref[:, :HEAD_DIM])
        value_ref[...] = pair_ref[:, HEAD_DIM:].astype(jnp.bfloat16)

    head = lax.axis_index("seq") * heads_here + pl.program_id(0)
    vert_live = vert_live_ref[head]
    slash_live = slash_live_ref[head]

    def listed(list_ref, live, slots, block):
        found = jnp.int32(0)
        for slot in range(slots):
            hit = (list_ref[head, slot] == block) & (live > slot)
            found = found | hit.astype(jnp.int32)
        return found

    vert_member = [listed(vert_ref, vert_live, VERT, block) for block in range(blocks)]
    slash_member = [listed(slash_ref, slash_live, SLASH, block) for block in range(blocks)]
    query = rotate(query_ref[...])
    causal = lax.broadcasted_iota(jnp.int32, (BLOCK, BLOCK), 1) <= lax.broadcasted_iota(
        jnp.int32, (BLOCK, BLOCK), 0
    )
    for row in range(blocks):
        width = (row + 1) * BLOCK
        scores = (
            lax.dot_general(
                query[row * BLOCK : width],
                key_ref[:width],
                (((1,), (1,)), ((), ())),
                preferred_element_type=jnp.float32,
            )
            * score_scale
        )
        masked = []
        for block in range(row + 1):
            visible = vert_member[block] | slash_member[row - block]
            bias = jnp.where(visible > 0, jnp.float32(0.0), jnp.float32(NEG_FILL))
            piece = scores[:, block * BLOCK : (block + 1) * BLOCK] + bias
            if block == row:
                piece = jnp.where(causal, piece, NEG_FILL)
            masked.append(piece)
        masked = masked[0] if row == 0 else jnp.concatenate(masked, axis=1)
        row_max = jnp.max(masked, axis=1, keepdims=True)
        weights = jnp.exp(masked - row_max)
        row_sum = jnp.sum(weights, axis=1, keepdims=True)
        weights_low = (weights / row_sum).astype(jnp.bfloat16)
        out_ref[row * BLOCK : width, :] = jnp.dot(
            weights_low, value_ref[:width], preferred_element_type=jnp.float32
        ).astype(jnp.bfloat16)


def attend(query_all, pair_all, cos_full, sin_full, lists):
    tokens, width = query_all.shape
    heads_here = width // HEAD_DIM
    whole = lambda head: (0, 0)
    one_head = lambda head: (0, head)
    return pl.pallas_call(
        functools.partial(attend_kernel, heads_here),
        grid=(heads_here,),
        out_shape=jax.ShapeDtypeStruct((tokens, width), jnp.bfloat16),
        in_specs=[
            pl.BlockSpec((tokens, HEAD_DIM), one_head),
            pl.BlockSpec((tokens, 2 * HEAD_DIM), whole),
            pl.BlockSpec((tokens, HEAD_DIM), whole),
            pl.BlockSpec((tokens, HEAD_DIM), whole),
        ]
        + [pl.BlockSpec(memory_space=pltpu.SMEM)] * 4,
        out_specs=pl.BlockSpec((tokens, HEAD_DIM), one_head),
        scratch_shapes=[
            pltpu.VMEM((tokens, HEAD_DIM), jnp.bfloat16),
            pltpu.VMEM((tokens, HEAD_DIM), jnp.bfloat16),
        ],
        compiler_params=pltpu.CompilerParams(vmem_limit_bytes=40 * 1024 * 1024),
    )(query_all, pair_all, cos_full, sin_full, *lists)


def swap_with(value, bit, size):
    return lax.ppermute(value, "seq", [(rank, rank ^ bit) for rank in range(size)])


def scatter_heads(segments, size, rank):
    bit = 1
    while bit < size:
        low = (rank // bit) % 2 == 0
        count = len(segments) // 2
        width = segments[0].shape[1]
        kept = [jnp.where(low, segments[2 * i], segments[2 * i + 1]) for i in range(count)]
        sent = [jnp.where(low, segments[2 * i + 1], segments[2 * i]) for i in range(count)]
        got = swap_with(jnp.concatenate(sent, axis=1), bit, size)
        segments = [kept[i] + got[:, i * width : (i + 1) * width] for i in range(count)]
        bit *= 2
    return segments[0]


def gather_heads(piece, size, rank):
    segments = [piece]
    width = piece.shape[1]
    bit = size // 2
    while bit >= 1:
        low = (rank // bit) % 2 == 0
        got = swap_with(jnp.concatenate(segments, axis=1), bit, size)
        wider = []
        for i, mine in enumerate(segments):
            other = got[:, i * width : (i + 1) * width]
            wider += [jnp.where(low, mine, other), jnp.where(low, other, mine)]
        segments = wider
        bit //= 2
    return jnp.concatenate(segments, axis=1)


def on_device(
    hidden, w_query, w_key, w_value, w_out, vert_blocks, vert_count, slash_offsets, slash_count
):
    seq_size = lax.axis_size("seq")
    seq_rank = lax.axis_index("seq")
    ring = lax.axis_size("tp")
    place = lax.axis_index("tp")
    rows = hidden.shape[0]
    tokens = rows * ring
    head_width = w_query.shape[1] // seq_size
    pairs = w_key.shape[1] // HEAD_DIM
    share = seq_size // pairs
    down = [(i, (i - 1) % ring) for i in range(ring)]
    up = [(i, (i + 1) % ring) for i in range(ring)]

    cos_table, sin_table = rope_tables(jnp.arange(tokens, dtype=jnp.int32))
    cos_full = jnp.repeat(cos_table, 2, axis=1)
    sin_full = jnp.stack([-sin_table, sin_table], axis=-1).reshape(tokens, HEAD_DIM)

    query_all = jnp.zeros((tokens, head_width), jnp.float32)
    pair_all = jnp.zeros((tokens, 2 * HEAD_DIM), jnp.float32)
    held = hidden
    for step in range(ring):
        later = lax.ppermute(held, "tp", down) if step < ring - 1 else None
        query = jnp.dot(held, w_query, preferred_element_type=jnp.float32)
        key = jnp.dot(held, w_key, preferred_element_type=jnp.float32)
        value = jnp.dot(held, w_value, preferred_element_type=jnp.float32)
        segments = []
        for segment in range(seq_size):
            pair = slice(segment // share * HEAD_DIM, (segment // share + 1) * HEAD_DIM)
            segments.append(
                jnp.concatenate(
                    [
                        query[:, segment * head_width : (segment + 1) * head_width],
                        key[:, pair],
                        value[:, pair],
                    ],
                    axis=1,
                )
            )
        mine = scatter_heads(segments, seq_size, seq_rank)
        start = (place + step) % ring * rows
        query_all = lax.dynamic_update_slice_in_dim(query_all, mine[:, :head_width], start, 0)
        pair_all = lax.dynamic_update_slice_in_dim(pair_all, mine[:, head_width:], start, 0)
        held = later

    attended = attend(
        query_all,
        pair_all,
        cos_full,
        sin_full,
        (vert_blocks, vert_count, slash_offsets, slash_count),
    )

    gathered = []
    for step in range(ring):
        start = (place + 2 * ring - 1 - step) % ring * rows
        piece = lax.dynamic_slice_in_dim(attended, start, rows, 0)
        gathered.append(gather_heads(piece, seq_size, seq_rank))
    got = None
    for step in range(ring):
        term = jnp.dot(gathered[step], w_out, preferred_element_type=jnp.float32)
        if step > 0:
            term = term + got.astype(jnp.float32)
        term = term.astype(jnp.bfloat16)
        if step < ring - 1:
            got = lax.ppermute(term, "tp", up)
    return term


def solution(mesh):
    in_specs = (
        P(("groups", "tp"), "seq"),
        P("seq", "tp"),
        P("seq", "tp"),
        P("seq", "tp"),
        P("tp", "seq"),
        P(("groups", "tp"), None),
        P(("groups", "tp")),
        P(("groups", "tp"), None),
        P(("groups", "tp")),
    )
    out_specs = P(("groups", "tp"), "seq")
    return jax.shard_map(
        on_device, mesh=mesh, in_specs=in_specs, out_specs=out_specs, check_vma=False
    )
```

time: 361 us -> 285 us (0.79)
  waiting for transfers between devices: 222 us -> 117 us
  matrix products: 72.7 us -> 116 us
  local copies, waits for them, and re-layouts: 28.9 us -> 7.12 us
  between operations: 13.4 us -> 0.86 us
  Pallas kernels: 0 us -> 11.5 us
  starting transfers between devices: 7.43 us -> 17 us
    ppermute x0 -> x22, waiting for transfers between devices: none -> 117 us  [the longest x3 56.2 us: on_device(): got = lax.ppermute(term, 'tp', up)]
    reduce_scatter x2 -> x0, waiting for transfers between devices: 114 us -> none  [the longest x1 60.4 us: on_device(): lax.psum_scatter(jnp.dot(gathered, w_out, preferred_element_type=jnp.floa...]
    all_gather x2 -> x0, waiting for transfers between devices: 96.3 us -> none  [the longest x1 67.9 us: on_device(): segment = lax.all_gather(hidden, 'tp', axis=0, tiled=True)]
    dot_general x16, matrix products: 72.7 us -> 116 us  [the longest x4 55.6 us: on_device(): term = jnp.dot(gathered[step], w_out, preferred_element_type=jnp.float32)]
    gather x48 -> x0, local copies, waits for them, and re-layouts: 18.7 us -> none  [the longest x30 7.04 us: slash_slot(): covered = jnp.take_along_axis(vert_member, safe_target, axis=1)]
    ppermute x0 -> x22, starting transfers between devices: none -> 17 us  [the longest x3 8.54 us: on_device(): later = lax.ppermute(held, 'tp', down) if step < ring - 1 else None]
    pallas_call x0 -> x1, Pallas kernels: none -> 11.5 us  [attend(): pl.pallas_call(functools.partial(attend_kernel, heads_here), grid=(heads_...]
    all_to_all x2 -> x0, waiting for transfers between devices: 11.3 us -> none  [the longest x1 11.3 us: on_device(): lax.all_to_all(query_rows, 'seq', split_axis=1, concat_axis=0, tiled=True)]
  transfers between devices with their start and end apart: 7 -> 22, of which waited for: 5 -> 13; matrix products, arithmetic and copies ran while one was open for 10% -> 36% of each run, Pallas kernels for 0% -> 0%
where the time goes in v1:
time: 285 us; the launch traced here: 284 us
  waiting for transfers between devices  117 us (41%)
  matrix products  116 us (41%)
  starting transfers between devices  17 us (6%)
  other arithmetic  14.8 us (5%)
  Pallas kernels  11.5 us (4%)
  local copies, waits for them, and re-layouts  7.12 us (2%)
    ppermute x3, waiting for transfers between devices, on_device(): got = lax.ppermute(term, 'tp', up)  56.2 us
    dot_general x4, matrix products, on_device(): term = jnp.dot(gathered[step], w_out, preferred_element_type=jnp.float32)  55.6 us
    dot_general x4, matrix products, on_device(): query = jnp.dot(held, w_query, preferred_element_type=jnp.float32)  53.9 us
    ppermute x16, waiting for transfers between devices, swap_with(): lax.ppermute(value, 'seq', [(rank, rank ^ bit) for rank in range(size)])  41.2 us
    ppermute x3, waiting for transfers between devices, on_device(): later = lax.ppermute(held, 'tp', down) if step < ring - 1 else None  19.9 us
    pallas_call x1, Pallas kernels, attend(): pl.pallas_call(functools.partial(attend_kernel, heads_here), grid=(heads_...  11.5 us
    ppermute x3, starting transfers between devices, on_device(): later = lax.ppermute(held, 'tp', down) if step < ring - 1 else None  8.54 us
    ppermute x16, starting transfers between devices, swap_with(): lax.ppermute(value, 'seq', [(rank, rank ^ bit) for rank in range(size)])  8.07 us
  transfers between devices with their start and end apart: 22, of which 13 were waited for; matrix products, arithmetic and copies ran while one was open for 36% of the time, Pallas kernels for 0%

profile of v1, /device:TPU:0, one launch (start us, length us, event | category | flops | bytes accessed | tf_op | source)
XLA Modules:
  0.0 284.2 jit_solution(17250941173146271207)
XLA Ops:
  0.0 5.0 %collective-permute-start.2 = (bf16[96,4096]{1,0:T(8,128)(2,1)}, bf16[96,4096]{1,0:T(8,128)(2,1)}, u32[]{:S(2)}, u32[]{:S(2)}) collective-permute-start(bf16[96,4096]{1,0:T(8,128)(2,1)} %param.9), channel_id=1, source_target_pairs={{0,3},{1,0},{2,1},{3,2},{4,7},{5,4},{6,5},{7,6},{8,11},{9,8},{10,9... | collective-permute-start | bytes 2359304 | tf_op jit(solution)/shard_map/ppermute | solution.py:191
  5.1 13.6 %fusion.56 = f32[96,4096]{1,0:T(8,128)S(1)} fusion(bf16[96,4096]{1,0:T(8,128)(2,1)} %param.9, bf16[4096,4096]{1,0:T(8,128)(2,1)} %param.10), kind=kOutput, calls=%fused_computation.158 | convolution fusion | flops 3221225472 | bytes 35913728 | tf_op jit(solution)/shard_map/dot_general | solution.py:192
  18.8 0.9 copy-done.6
  20.3 1.7 copy-done.4
  22.6 1.1 pad_maximum_fusion
  25.5 13.6 %fusion.59 = f32[96,4096]{1,0:T(8,128)S(1)} fusion(bf16[96,4096]{1,0:T(8,128)(2,1)} %collective-permute-done.2, bf16[4096,4096]{1,0:T(8,128)(2,1)} %param.10), kind=kOutput, calls=%fused_computation.161 | convolution fusion | flops 3221225472 | bytes 35913728 | tf_op jit(solution)/shard_map/dot_general | solution.py:192
  39.1 1.8 fusion.60
  40.9 1.6 fusion.61
  42.8 0.8 copy-done.8
  44.0 1.4 broadcast_select_fusion.3
  45.5 1.6 collective-permute-start.1
  47.2 1.0 pad_maximum_fusion.1
  48.4 0.7 collective-permute-start.5
  49.2 10.0 %collective-permute-done.1 = f32[96,1280]{1,0:T(8,128)S(1)} collective-permute-done((f32[96,1280]{1,0:T(8,128)S(1)}, f32[96,1280]{1,0:T(8,128)S(1)}, u32[]{:S(2)}, u32[]{:S(2)}) %collective-permute-start.1) | collective-permute-done | bytes 491552 | tf_op jit(solution)/shard_map/ppermute | solution.py:135
  59.2 1.4 select_add_fusion.3
  60.9 7.5 %collective-permute-done.5 = bf16[96,4096]{1,0:T(8,128)(2,1)S(1)} collective-permute-done((bf16[96,4096]{1,0:T(8,128)(2,1)}, bf16[96,4096]{1,0:T(8,128)(2,1)S(1)}, u32[]{:S(2)}, u32[]{:S(2)}) %collective-permute-start.5) | collective-permute-done | bytes 786464 | tf_op jit(solution)/shard_map/ppermute | solution.py:191
  68.9 13.4 %fusion.62 = f32[96,4096]{1,0:T(8,128)S(1)} fusion(bf16[96,4096]{1,0:T(8,128)(2,1)S(1)} %collective-permute-done.5, bf16[4096,4096]{1,0:T(8,128)(2,1)} %param.10), kind=kOutput, calls=%fused_computation.164 | convolution fusion | flops 3221225472 | bytes 35913728 | tf_op jit(solution)/shard_map/dot_general | solution.py:192
  82.8 2.8 collective-permute-start.8
  85.9 1.0 pad_maximum_fusion.2
  87.2 2.2 broadcast_select_fusion.2
  89.4 0.5 collective-permute-start.4
  89.9 12.4 %collective-permute-done.8 = bf16[96,4096]{1,0:T(8,128)(2,1)S(1)} collective-permute-done((bf16[96,4096]{1,0:T(8,128)(2,1)S(1)}, bf16[96,4096]{1,0:T(8,128)(2,1)S(1)}, u32[]{:S(2)}, u32[]{:S(2)}) %collective-permute-start.8) | collective-permute-done | bytes 786464 | tf_op jit(solution)/shard_map/ppermute | solution.py:191
  102.2 13.4 %fusion.65 = f32[96,4096]{1,0:T(8,128)S(1)} fusion(bf16[96,4096]{1,0:T(8,128)(2,1)S(1)} %collective-permute-done.8, bf16[4096,4096]{1,0:T(8,128)(2,1)} %param.10), kind=kOutput, calls=%fused_computation.167 | convolution fusion | flops 3221225472 | bytes 35913728 | tf_op jit(solution)/shard_map/dot_general | solution.py:192
  117.1 0.8 copy-done.17
  117.9 1.6 select_add_fusion.2
  119.5 1.4 broadcast_select_fusion.1
  120.9 0.6 collective-permute-start.7
  121.7 1.6 collective-permute-start.10
  123.3 11.8 %collective-permute-done.7 = f32[96,1280]{1,0:T(8,128)S(1)} collective-permute-done((f32[96,1280]{1,0:T(8,128)S(1)}, f32[96,1280]{1,0:T(8,128)S(1)}, u32[]{:S(2)}, u32[]{:S(2)}) %collective-permute-start.7) | collective-permute-done | bytes 491552 | tf_op jit(solution)/shard_map/ppermute | solution.py:135
  135.1 1.4 select_add_fusion.1
  136.6 7.8 %collective-permute-done.10 = f32[96,1280]{1,0:T(8,128)S(1)} collective-permute-done((f32[96,1280]{1,0:T(8,128)S(1)}, f32[96,1280]{1,0:T(8,128)S(1)}, u32[]{:S(2)}, u32[]{:S(2)}) %collective-permute-start.10) | collective-permute-done | bytes 491552 | tf_op jit(solution)/shard_map/ppermute | solution.py:135
  144.6 11.5 %shard_map.91 = bf16[384,1024]{1,0:T(8,128)(2,1)S(1)} custom-call(f32[384,1024]{1,0:T(8,128)S(1)} %slice_dynamic-update-slice_fusion.query_ref, f32[384,256]{1,0:T(8,128)S(1)} %slice_dynamic-update-slice_fusion.4.pair_ref, f32[384,128]{1,0:T(8,128)S(1)} %copy.17.cos_ref, f32[384,128]{1,0:T(8,128)S(1)} %copy.18.sin_ref, s32[32,3]{1,0:T(8,128)S(1)} %copy.19.vert_ref, ...), custom_call_target="tpu_custom_call" | custom-call | tf_op jit(solution)/shard_map/pallas_call | solution.py:114
  156.2 0.6 collective-permute-start.17
  156.8 1.5 collective-permute-start.15
  158.3 5.7 %collective-permute-done.17 = bf16[96,1024]{1,0:T(8,128)(2,1)S(1)} collective-permute-done((bf16[96,1024]{1,0:T(8,128)(2,1)S(1)}, bf16[96,1024]{1,0:T(8,128)(2,1)S(1)}, u32[]{:S(2)}, u32[]{:S(2)}) %collective-permute-start.17) | collective-permute-done | bytes 196640 | tf_op jit(solution)/shard_map/ppermute | solution.py:135
  164.2 0.6 collective-permute-start.13
  164.8 1.4 collective-permute-done.15
  166.2 13.6 %convolution_convert_fusion = bf16[96,4096]{1,0:T(8,128)(2,1)S(1)} fusion(bf16[4096,4096]{1,0:T(8,128)(2,1)} %param.13, bf16[96,1024]{1,0:T(8,128)(2,1)S(1)} %get-tuple-element.53, bf16[96,1024]{1,0:T(8,128)(2,1)S(1)} %get-tuple-element.54, bf16[96,1024]{1,0:T(8,128)(2,1)S(1)} %get-tuple-element.38, bf16[96,1024]{1,0:T(8,128)(2,1)S(1)} %get-tuple-element.37), kind=kOutput, calls=%fused_computation.6 | convolution fusion | flops 3224764416 | bytes 35127296 | tf_op jit(solution)/shard_map/dot_general | solution.py:229
  180.2 0.6 collective-permute-start.11
  180.8 1.1 collective-permute-done.16
  182.0 19.9 %collective-permute-done.19 = bf16[96,4096]{1,0:T(8,128)(2,1)S(1)} collective-permute-done((bf16[96,4096]{1,0:T(8,128)(2,1)S(1)}, bf16[96,4096]{1,0:T(8,128)(2,1)S(1)}, u32[]{:S(2)}, u32[]{:S(2)}) %collective-permute-start.19) | collective-permute-done | bytes 786464 | tf_op jit(solution)/shard_map/ppermute | solution.py:234
  201.9 13.7 %fusion.2 = bf16[96,4096]{1,0:T(8,128)(2,1)S(1)} fusion(bf16[4096,4096]{1,0:T(8,128)(2,1)} %param.13, bf16[96,4096]{1,0:T(8,128)(2,1)S(1)} %collective-permute-done.19, bf16[96,1024]{1,0:T(8,128)(2,1)S(1)} %get-tuple-element.49, bf16[96,1024]{1,0:T(8,128)(2,1)S(1)} %get-tuple-element.50, bf16[96,1024]{1,0:T(8,128)(2,1)S(1)} %get-tuple-element.34, ...), kind=kOutput, calls=%fused_computation.5 | convolution fusion | flops 3225550848 | bytes 35913728 | tf_op jit(solution)/shard_map/dot_general | solution.py:229
  215.8 1.7 collective-permute-done.14
  217.5 18.6 %collective-permute-done.20 = bf16[96,4096]{1,0:T(8,128)(2,1)S(1)} collective-permute-done((bf16[96,4096]{1,0:T(8,128)(2,1)S(1)}, bf16[96,4096]{1,0:T(8,128)(2,1)S(1)}, u32[]{:S(2)}, u32[]{:S(2)}) %collective-permute-start.20) | collective-permute-done | bytes 786464 | tf_op jit(solution)/shard_map/ppermute | solution.py:234
  236.2 13.7 %fusion.1 = bf16[96,4096]{1,0:T(8,128)(2,1)S(1)} fusion(bf16[4096,4096]{1,0:T(8,128)(2,1)} %param.13, bf16[96,4096]{1,0:T(8,128)(2,1)S(1)} %collective-permute-done.20, bf16[96,1024]{1,0:T(8,128)(2,1)S(1)} %get-tuple-element.45, bf16[96,1024]{1,0:T(8,128)(2,1)S(1)} %get-tuple-element.46, bf16[96,1024]{1,0:T(8,128)(2,1)S(1)} %get-tuple-element.30, ...), kind=kOutput, calls=%fused_computation.4 | convolution fusion | flops 3225550848 | bytes 35913728 | tf_op jit(solution)/shard_map/dot_general | solution.py:229
  250.0 1.7 collective-permute-done.12
  251.8 17.7 %collective-permute-done.21 = bf16[96,4096]{1,0:T(8,128)(2,1)S(1)} collective-permute-done((bf16[96,4096]{1,0:T(8,128)(2,1)S(1)}, bf16[96,4096]{1,0:T(8,128)(2,1)S(1)}, u32[]{:S(2)}, u32[]{:S(2)}) %collective-permute-start.21) | collective-permute-done | bytes 786464 | tf_op jit(solution)/shard_map/ppermute | solution.py:234
  269.5 14.7 %fusion = bf16[96,4096]{1,0:T(8,128)(2,1)} fusion(bf16[4096,4096]{1,0:T(8,128)(2,1)} %param.13, bf16[96,4096]{1,0:T(8,128)(2,1)S(1)} %collective-permute-done.21, bf16[96,1024]{1,0:T(8,128)(2,1)S(1)} %get-tuple-element.41, bf16[96,1024]{1,0:T(8,128)(2,1)S(1)} %get-tuple-element.42, bf16[96,1024]{1,0:T(8,128)(2,1)S(1)} %get-tuple-element.26, ...), kind=kOutput, calls=%fused_computation.3 | convolution fusion | flops 3225550848 | bytes 35913728 | tf_op jit(solution)/shard_map/dot_general | solution.py:229
  (133 shorter events, 9.1 us)
Async XLA Ops:
  0.0 18.8 %copy-start = (bf16[4096,256]{1,0:T(8,128)(2,1)S(1)}, bf16[4096,256]{1,0:T(8,128)(2,1)}, u32[]{:S(2)}) copy-start(bf16[4096,256]{1,0:T(8,128)(2,1)} %param.11) | copy-start | bytes 6291460
  0.0 25.5 %collective-permute-start.2 = (bf16[96,4096]{1,0:T(8,128)(2,1)}, bf16[96,4096]{1,0:T(8,128)(2,1)}, u32[]{:S(2)}, u32[]{:S(2)}) collective-permute-start(bf16[96,4096]{1,0:T(8,128)(2,1)} %param.9), channel_id=1, source_target_pairs={{0,3},{1,0},{2,1},{3,2},{4,7},{5,4},{6,5},{7,6},{8,11},{9,8},{10,9... | collective-permute-start | bytes 2359304 | tf_op jit(solution)/shard_map/ppermute | solution.py:191
  18.6 1.1 copy-start.6
  19.8 2.7 copy-start.7
  19.8 2.7 copy-start.9
  19.8 2.7 copy-start.11
  19.8 2.7 copy-start.13
  19.8 2.2 copy-start.4
  23.7 19.1 %collective-permute-start = (f32[96,2560]{1,0:T(8,128)}, f32[96,2560]{1,0:T(8,128)}, u32[]{:S(2)}, u32[]{:S(2)}) collective-permute-start(f32[96,2560]{1,0:T(8,128)} %pad_maximum_fusion), channel_id=1, source_target_pairs={{0,4},{4,0},{8,12},{12,8},{1,5},{5,1},{9,13},{13,9},{2,6},{6,2},{1... | collective-permute-start | bytes 2949128 | tf_op jit(solution)/shard_map/ppermute | solution.py:135
  23.7 1.7 copy-start.26
  23.7 1.8 copy-start.27
  39.1 1.8 copy-start.5
  42.6 1.1 copy-start.10
  42.6 1.4 copy-start.12
  42.6 1.5 copy-start.14
  42.8 4.3 %copy-start.15 = (f32[96,1024]{1,0:T(8,128)}, f32[96,1024]{1,0:T(8,128)S(1)}, u32[]{:S(2)}) copy-start(f32[96,1024]{1,0:T(8,128)S(1)} %get-tuple-element.16) | copy-start | bytes 1179652
  45.5 13.7 %collective-permute-start.1 = (f32[96,1280]{1,0:T(8,128)S(1)}, f32[96,1280]{1,0:T(8,128)S(1)}, u32[]{:S(2)}, u32[]{:S(2)}) collective-permute-start(f32[96,1280]{1,0:T(8,128)S(1)} %broadcast_select_fusion.3), channel_id=1, source_target_pairs={{0,8},{4,12},{8,0},{12,4},{1,9},{5,13},{9,1},{13,5},{2,10},{6,14},... | collective-permute-start | bytes 1474568 | tf_op jit(solution)/shard_map/ppermute | solution.py:135
  48.2 39.0 %collective-permute-start.3 = (f32[96,2560]{1,0:T(8,128)}, f32[96,2560]{1,0:T(8,128)}, u32[]{:S(2)}, u32[]{:S(2)}) collective-permute-start(f32[96,2560]{1,0:T(8,128)} %pad_maximum_fusion.1), channel_id=1, source_target_pairs={{0,4},{4,0},{8,12},{12,8},{1,5},{5,1},{9,13},{13,9},{2,6},{6,2},{1... | collective-permute-start | bytes 2949128 | tf_op jit(solution)/shard_map/ppermute | solution.py:135
  48.4 19.9 %collective-permute-start.5 = (bf16[96,4096]{1,0:T(8,128)(2,1)}, bf16[96,4096]{1,0:T(8,128)(2,1)S(1)}, u32[]{:S(2)}, u32[]{:S(2)}) collective-permute-start(bf16[96,4096]{1,0:T(8,128)(2,1)} %collective-permute-done.2), channel_id=1, source_target_pairs={{0,3},{1,0},{2,1},{3,2},{4,7},{5,4},{6,5},{7,6},{8,11},{9,8},{10,9... | collective-permute-start | bytes 2359304 | tf_op jit(solution)/shard_map/ppermute | solution.py:191
  82.8 19.5 %collective-permute-start.8 = (bf16[96,4096]{1,0:T(8,128)(2,1)S(1)}, bf16[96,4096]{1,0:T(8,128)(2,1)S(1)}, u32[]{:S(2)}, u32[]{:S(2)}) collective-permute-start(bf16[96,4096]{1,0:T(8,128)(2,1)S(1)} %collective-permute-done.5), channel_id=1, source_target_pairs={{0,3},{1,0},{2,1},{3,2},{4,7},{5,4},{6,5},{7,6},{8,11},{9,8},{10,9... | collective-permute-start | bytes 2359304 | tf_op jit(solution)/shard_map/ppermute | solution.py:191
  85.7 1.2 copy-start.18
  85.7 1.2 copy-start.20
  85.7 1.3 copy-start.22
  85.8 1.4 copy-start.24
  85.9 1.3 copy-start.16
  87.2 32.3 %collective-permute-start.6 = (f32[96,2560]{1,0:T(8,128)}, f32[96,2560]{1,0:T(8,128)}, u32[]{:S(2)}, u32[]{:S(2)}) collective-permute-start(f32[96,2560]{1,0:T(8,128)} %pad_maximum_fusion.2), channel_id=1, source_target_pairs={{0,4},{4,0},{8,12},{12,8},{1,5},{5,1},{9,13},{13,9},{2,6},{6,2},{1... | collective-permute-start | bytes 2949128 | tf_op jit(solution)/shard_map/ppermute | solution.py:135
  89.4 27.7 %collective-permute-start.4 = (f32[96,1280]{1,0:T(8,128)}, f32[96,1280]{1,0:T(8,128)}, u32[]{:S(2)}, u32[]{:S(2)}) collective-permute-start(f32[96,1280]{1,0:T(8,128)} %broadcast_select_fusion.2), channel_id=1, source_target_pairs={{0,8},{4,12},{8,0},{12,4},{1,9},{5,13},{9,1},{13,5},{2,10},{6,14},... | collective-permute-start | bytes 1474568 | tf_op jit(solution)/shard_map/ppermute | solution.py:135
  117.0 2.5 copy-start.19
  117.0 2.5 copy-start.21
  117.0 2.5 copy-start.23
  117.0 2.5 copy-start.25
  117.0 4.5 %collective-permute-start.9 = (f32[96,2560]{1,0:T(8,128)S(1)}, f32[96,2560]{1,0:T(8,128)S(1)}, u32[]{:S(2)}, u32[]{:S(2)}) collective-permute-start(f32[96,2560]{1,0:T(8,128)S(1)} %pad_maximum_fusion.3), channel_id=1, source_target_pairs={{0,4},{4,0},{8,12},{12,8},{1,5},{5,1},{9,13},{13,9},{2,6},{6,2},{1... | collective-permute-start | bytes 2949128 | tf_op jit(solution)/shard_map/ppermute | solution.py:135
  120.9 14.2 %collective-permute-start.7 = (f32[96,1280]{1,0:T(8,128)S(1)}, f32[96,1280]{1,0:T(8,128)S(1)}, u32[]{:S(2)}, u32[]{:S(2)}) collective-permute-start(f32[96,1280]{1,0:T(8,128)S(1)} %broadcast_select_fusion.1), channel_id=1, source_target_pairs={{0,8},{4,12},{8,0},{12,4},{1,9},{5,13},{9,1},{13,5},{2,10},{6,14},... | collective-permute-start | bytes 1474568 | tf_op jit(solution)/shard_map/ppermute | solution.py:135
  121.7 22.7 %collective-permute-start.10 = (f32[96,1280]{1,0:T(8,128)S(1)}, f32[96,1280]{1,0:T(8,128)S(1)}, u32[]{:S(2)}, u32[]{:S(2)}) collective-permute-start(f32[96,1280]{1,0:T(8,128)S(1)} %broadcast_select_fusion), channel_id=1, source_target_pairs={{0,8},{4,12},{8,0},{12,4},{1,9},{5,13},{9,1},{13,5},{2,10},{6,14},... | collective-permute-start | bytes 1474568 | tf_op jit(solution)/shard_map/ppermute | solution.py:135
  136.6 8.1 %copy-start.2 = (s32[32]{0:T(128)S(1)}, s32[32]{0:T(128)}, u32[]{:S(2)}) copy-start(s32[32]{0:T(128)} %vert_live_ref.1) | copy-start | bytes 388
  136.6 8.1 %copy-start.3 = (s32[32]{0:T(128)S(1)}, s32[32]{0:T(128)}, u32[]{:S(2)}) copy-start(s32[32]{0:T(128)} %slash_live_ref.1) | copy-start | bytes 388
  156.2 7.8 %collective-permute-start.17 = (bf16[96,1024]{1,0:T(8,128)(2,1)S(1)}, bf16[96,1024]{1,0:T(8,128)(2,1)S(1)}, u32[]{:S(2)}, u32[]{:S(2)}) collective-permute-start(bf16[96,1024]{1,0:T(8,128)(2,1)S(1)} %get-tuple-element.22), channel_id=1, source_target_pairs={{0,8},{4,12},{8,0},{12,4},{1,9},{5,13},{9,1},{13,5},{2,10},{6,14},... | collective-permute-start | bytes 589832 | tf_op jit(solution)/shard_map/ppermute | solution.py:135
  156.8 9.3 %collective-permute-start.15 = (bf16[96,1024]{1,0:T(8,128)(2,1)S(1)}, bf16[96,1024]{1,0:T(8,128)(2,1)S(1)}, u32[]{:S(2)}, u32[]{:S(2)}) collective-permute-start(bf16[96,1024]{1,0:T(8,128)(2,1)S(1)} %get-tuple-element.23), channel_id=1, source_target_pairs={{0,8},{4,12},{8,0},{12,4},{1,9},{5,13},{9,1},{13,5},{2,10},{6,14},... | collective-permute-start | bytes 589832 | tf_op jit(solution)/shard_map/ppermute | solution.py:135
  164.1 2.1 collective-permute-start.18
  164.2 16.6 %collective-permute-start.13 = (bf16[96,1024]{1,0:T(8,128)(2,1)S(1)}, bf16[96,1024]{1,0:T(8,128)(2,1)S(1)}, u32[]{:S(2)}, u32[]{:S(2)}) collective-permute-start(bf16[96,1024]{1,0:T(8,128)(2,1)S(1)} %get-tuple-element.24), channel_id=1, source_target_pairs={{0,8},{4,12},{8,0},{12,4},{1,9},{5,13},{9,1},{13,5},{2,10},{6,14},... | collective-permute-start | bytes 589832 | tf_op jit(solution)/shard_map/ppermute | solution.py:135
  179.8 22.1 %collective-permute-start.19 = (bf16[96,4096]{1,0:T(8,128)(2,1)S(1)}, bf16[96,4096]{1,0:T(8,128)(2,1)S(1)}, u32[]{:S(2)}, u32[]{:S(2)}) collective-permute-start(bf16[96,4096]{1,0:T(8,128)(2,1)S(1)} %convolution_convert_fusion), channel_id=1, source_target_pairs={{0,1},{1,2},{2,3},{3,0},{4,5},{5,6},{6,7},{7,4},{8,9},{9,10},{10,1... | collective-permute-start | bytes 2359304 | tf_op jit(solution)/shard_map/ppermute | solution.py:234
  180.2 1.8 collective-permute-start.16
  180.2 35.5 %collective-permute-start.11 = (bf16[96,1024]{1,0:T(8,128)(2,1)S(1)}, bf16[96,1024]{1,0:T(8,128)(2,1)S(1)}, u32[]{:S(2)}, u32[]{:S(2)}) collective-permute-start(bf16[96,1024]{1,0:T(8,128)(2,1)S(1)} %get-tuple-element.21), channel_id=1, source_target_pairs={{0,8},{4,12},{8,0},{12,4},{1,9},{5,13},{9,1},{13,5},{2,10},{6,14},... | collective-permute-start | bytes 589832 | tf_op jit(solution)/shard_map/ppermute | solution.py:135
  215.6 20.6 %collective-permute-start.20 = (bf16[96,4096]{1,0:T(8,128)(2,1)S(1)}, bf16[96,4096]{1,0:T(8,128)(2,1)S(1)}, u32[]{:S(2)}, u32[]{:S(2)}) collective-permute-start(bf16[96,4096]{1,0:T(8,128)(2,1)S(1)} %fusion.2), channel_id=1, source_target_pairs={{0,1},{1,2},{2,3},{3,0},{4,5},{5,6},{6,7},{7,4},{8,9},{9,10},{10,1... | collective-permute-start | bytes 2359304 | tf_op jit(solution)/shard_map/ppermute | solution.py:234
  215.7 1.8 collective-permute-start.14
  249.8 19.7 %collective-permute-start.21 = (bf16[96,4096]{1,0:T(8,128)(2,1)S(1)}, bf16[96,4096]{1,0:T(8,128)(2,1)S(1)}, u32[]{:S(2)}, u32[]{:S(2)}) collective-permute-start(bf16[96,4096]{1,0:T(8,128)(2,1)S(1)} %fusion.1), channel_id=1, source_target_pairs={{0,1},{1,2},{2,3},{3,0},{4,5},{5,6},{6,7},{7,4},{8,9},{9,10},{10,1... | collective-permute-start | bytes 2359304 | tf_op jit(solution)/shard_map/ppermute | solution.py:234
  249.9 1.8 collective-permute-start.12
  269.5 14.7 %copy-start.1 = (bf16[4096,256]{1,0:T(8,128)(2,1)S(1)}, bf16[4096,256]{1,0:T(8,128)(2,1)}, u32[]{:S(2)}) copy-start(bf16[4096,256]{1,0:T(8,128)(2,1)} %param.11) | copy-start | bytes 6291460
  (2 other events, 2.0 us)

commit v2 on v1

--- a/solution.py
+++ b/solution.py
@@ -12,6 +12,7 @@
 BLOCK = 128
 VERT = 3
 SLASH = 3
+PARTS = 2
 
 
 NEG_FILL = -1e30
@@ -135,33 +136,36 @@
     return lax.ppermute(value, "seq", [(rank, rank ^ bit) for rank in range(size)])
 
 
-def scatter_heads(segments, size, rank):
-    bit = 1
-    while bit < size:
-        low = (rank // bit) % 2 == 0
-        count = len(segments) // 2
-        width = segments[0].shape[1]
-        kept = [jnp.where(low, segments[2 * i], segments[2 * i + 1]) for i in range(count)]
-        sent = [jnp.where(low, segments[2 * i + 1], segments[2 * i]) for i in range(count)]
-        got = swap_with(jnp.concatenate(sent, axis=1), bit, size)
-        segments = [kept[i] + got[:, i * width : (i + 1) * width] for i in range(count)]
-        bit *= 2
-    return segments[0]
-
-
-def gather_heads(piece, size, rank):
-    segments = [piece]
-    width = piece.shape[1]
+def halve(segments, bit, size, rank):
+    low = (rank // bit) % 2 == 0
+    count = len(segments) // 2
+    kept = [jnp.where(low, segments[2 * i], segments[2 * i + 1]) for i in range(count)]
+    sent = [jnp.where(low, segments[2 * i + 1], segments[2 * i]) for i in range(count)]
+    return kept, swap_with(jnp.concatenate(sent, axis=1), bit, size)
+
+
+def join_halves(kept, got):
+    width = kept[0].shape[1]
+    return [mine + got[:, i * width : (i + 1) * width] for i, mine in enumerate(kept)]
+
+
+def widen(segments, got, bit, rank):
+    low = (rank // bit) % 2 == 0
+    width = segments[0].shape[1]
+    wider = []
+    for i, mine in enumerate(segments):
+        other = got[:, i * width : (i + 1) * width]
+        wider += [jnp.where(low, mine, other), jnp.where(low, other, mine)]
+    return wider
+
+
+def gather_rest(piece, got, size, rank):
     bit = size // 2
-    while bit >= 1:
-        low = (rank // bit) % 2 == 0
+    segments = widen([piece], got, bit, rank)
+    while bit > 1:
+        bit //= 2
         got = swap_with(jnp.concatenate(segments, axis=1), bit, size)
-        wider = []
-        for i, mine in enumerate(segments):
-            other = got[:, i * width : (i + 1) * width]
-            wider += [jnp.where(low, mine, other), jnp.where(low, other, mine)]
-        segments = wider
-        bit //= 2
+        segments = widen(segments, got, bit, rank)
     return jnp.concatenate(segments, axis=1)
 
 
@@ -186,30 +190,51 @@
 
     query_all = jnp.zeros((tokens, head_width), jnp.float32)
     pair_all = jnp.zeros((tokens, 2 * HEAD_DIM), jnp.float32)
+    stages = [1 << i for i in range(seq_size.bit_length() - 1)]
+    flying = []
+    done = [None] * ring
     held = hidden
-    for step in range(ring):
-        later = lax.ppermute(held, "tp", down) if step < ring - 1 else None
-        query = jnp.dot(held, w_query, preferred_element_type=jnp.float32)
-        key = jnp.dot(held, w_key, preferred_element_type=jnp.float32)
-        value = jnp.dot(held, w_value, preferred_element_type=jnp.float32)
-        segments = []
-        for segment in range(seq_size):
-            pair = slice(segment // share * HEAD_DIM, (segment // share + 1) * HEAD_DIM)
-            segments.append(
-                jnp.concatenate(
-                    [
-                        query[:, segment * head_width : (segment + 1) * head_width],
-                        key[:, pair],
-                        value[:, pair],
-                    ],
-                    axis=1,
+    for step in range(ring + len(stages)):
+        query = None
+        if step < ring:
+            later = lax.ppermute(held, "tp", down) if step < ring - 1 else None
+            query = jnp.dot(held, w_query, preferred_element_type=jnp.float32)
+            key = jnp.dot(held, w_key, preferred_element_type=jnp.float32)
+            value = jnp.dot(held, w_value, preferred_element_type=jnp.float32)
+            if flying:
+                landed, query = lax.optimization_barrier(([entry[3] for entry in flying], query))
+                flying = [entry[:3] + (got,) for entry, got in zip(flying, landed)]
+        moved = []
+        for block, stage, kept, got in flying:
+            segments = join_halves(kept, got)
+            if stage + 1 < len(stages):
+                moved.append((block, stage + 1, segments))
+            else:
+                done[block] = segments[0]
+        if query is not None:
+            segments = []
+            for segment in range(seq_size):
+                pair = slice(segment // share * HEAD_DIM, (segment // share + 1) * HEAD_DIM)
+                segments.append(
+                    jnp.concatenate(
+                        [
+                            query[:, segment * head_width : (segment + 1) * head_width],
+                            key[:, pair],
+                            value[:, pair],
+                        ],
+                        axis=1,
+                    )
                 )
-            )
-        mine = scatter_heads(segments, seq_size, seq_rank)
+            moved.append((step, 0, segments))
+            held = later
+        flying = []
+        for block, stage, segments in moved:
+            kept, got = halve(segments, stages[stage], seq_size, seq_rank)
+            flying.append((block, stage, kept, got))
+    for step, mine in enumerate(done):
         start = (place + step) % ring * rows
         query_all = lax.dynamic_update_slice_in_dim(query_all, mine[:, :head_width], start, 0)
         pair_all = lax.dynamic_update_slice_in_dim(pair_all, mine[:, head_width:], start, 0)
-        held = later
 
     attended = attend(
         query_all,
@@ -219,20 +244,37 @@
         (vert_blocks, vert_count, slash_offsets, slash_count),
     )
 
-    gathered = []
+    pieces, halfway = [], []
     for step in range(ring):
         start = (place + 2 * ring - 1 - step) % ring * rows
-        piece = lax.dynamic_slice_in_dim(attended, start, rows, 0)
-        gathered.append(gather_heads(piece, seq_size, seq_rank))
-    got = None
+        pieces.append(lax.dynamic_slice_in_dim(attended, start, rows, 0))
+        halfway.append(swap_with(pieces[step], seq_size // 2, seq_size))
+    columns = w_out.shape[1] // PARTS
+    got = [None] * PARTS
+    gathered = gather_rest(pieces[0], halfway[0], seq_size, seq_rank)
     for step in range(ring):
-        term = jnp.dot(gathered[step], w_out, preferred_element_type=jnp.float32)
-        if step > 0:
-            term = term + got.astype(jnp.float32)
-        term = term.astype(jnp.bfloat16)
-        if step < ring - 1:
-            got = lax.ppermute(term, "tp", up)
-    return term
+        terms = []
+        for part in range(PARTS):
+            term = jnp.dot(
+                gathered,
+                w_out[:, part * columns : (part + 1) * columns],
+                preferred_element_type=jnp.float32,
+            )
+            if part == 0 and step + 1 < ring:
+                landed, term = lax.optimization_barrier((halfway[step + 1], term))
+                following = gather_rest(pieces[step + 1], landed, seq_size, seq_rank)
+            if step > 0:
+                term, arrived = lax.optimization_barrier((term, got[part]))
+                term = term + arrived.astype(jnp.float32)
+            term = term.astype(jnp.bfloat16)
+            if part + 1 < PARTS:
+                gathered, term = lax.optimization_barrier((gathered, term))
+            elif step + 1 < ring:
+                gathered, term = lax.optimization_barrier((following, term))
+            terms.append(term)
+            if step < ring - 1:
+                got[part] = lax.ppermute(term, "tp", up)
+    return jnp.concatenate(terms, axis=1)
 
 
 def solution(mesh):

time: 285 us -> 246 us (0.86)
  waiting for transfers between devices: 117 us -> 70.1 us
  matrix products: 116 us -> 120 us
  starting transfers between devices: 17 us -> 20.7 us
    ppermute x3 -> x6, waiting for transfers between devices: 56.2 us -> 23.9 us  [on_device(): got[part] = lax.ppermute(term, 'tp', up)]
    ppermute x16, waiting for transfers between devices: 41.2 us -> 26.7 us  [swap_with(): lax.ppermute(value, 'seq', [(rank, rank ^ bit) for rank in range(size)])]
    ppermute x16, starting transfers between devices: 8.07 us -> 11.3 us  [swap_with(): lax.ppermute(value, 'seq', [(rank, rank ^ bit) for rank in range(size)])]
    dot_general x4 -> x8, matrix products: 55.6 us -> 58.5 us  [on_device(): jnp.dot(gathered, w_out[:, part * columns:(part + 1) * columns], preferre...]
    unnamed x58 -> x86, local copies, waits for them, and re-layouts: 5.22 us -> 2.33 us
    select_n x16 -> x19, other arithmetic: 5.97 us -> 6.93 us  [the longest x11 6.57 us: halve(): jnp.where(low, segments[2 * i + 1], segments[2 * i])]
  transfers between devices with their start and end apart: 22 -> 25, of which waited for: 13 -> 11; matrix products, arithmetic and copies ran while one was open for 36% -> 56% of each run, Pallas kernels for 0% -> 0%
where the time goes in v2:
time: 246 us
  matrix products  120 us (49%)
  waiting for transfers between devices  70.1 us (28%)
  starting transfers between devices  20.7 us (8%)
  other arithmetic  17.2 us (7%)
  Pallas kernels  11.5 us (5%)
  local copies, waits for them, and re-layouts  4.88 us (2%)
    dot_general x8, matrix products, on_device(): jnp.dot(gathered, w_out[:, part * columns:(part + 1) * columns], preferre...  58.5 us
    dot_general x4, matrix products, on_device(): query = jnp.dot(held, w_query, preferred_element_type=jnp.float32)  53.7 us
    ppermute x16, waiting for transfers between devices, swap_with(): lax.ppermute(value, 'seq', [(rank, rank ^ bit) for rank in range(size)])  26.7 us
    ppermute x6, waiting for transfers between devices, on_device(): got[part] = lax.ppermute(term, 'tp', up)  23.9 us
    ppermute x3, waiting for transfers between devices, on_device(): later = lax.ppermute(held, 'tp', down) if step < ring - 1 else None  19.5 us
    pallas_call x1, Pallas kernels, attend(): pl.pallas_call(functools.partial(attend_kernel, heads_here), grid=(heads_...  11.5 us
    ppermute x16, starting transfers between devices, swap_with(): lax.ppermute(value, 'seq', [(rank, rank ^ bit) for rank in range(size)])  11.3 us
    ppermute x3, starting transfers between devices, on_device(): later = lax.ppermute(held, 'tp', down) if step < ring - 1 else None  8.47 us
  transfers between devices with their start and end apart: 25, of which 11 were waited for; matrix products, arithmetic and copies ran while one was open for 56% of the time, Pallas kernels for 0%

profile of v2, /device:TPU:0, one launch (start us, length us, event | category | flops | bytes accessed | tf_op | source)
XLA Modules:
  0.0 245.9 jit_solution(5594569617702280419)
XLA Ops:
  0.0 5.0 %collective-permute-start.1 = (bf16[96,4096]{1,0:T(8,128)(2,1)}, bf16[96,4096]{1,0:T(8,128)(2,1)}, u32[]{:S(2)}, u32[]{:S(2)}) collective-permute-start(bf16[96,4096]{1,0:T(8,128)(2,1)} %param.9), channel_id=1, source_target_pairs={{0,3},{1,0},{2,1},{3,2},{4,7},{5,4},{6,5},{7,6},{8,11},{9,8},{10,9... | collective-permute-start | bytes 2359304 | tf_op jit(solution)/shard_map/ppermute | solution.py:200
  5.1 2.3 fusion.42
  7.9 13.4 %fusion.40 = f32[96,4096]{1,0:T(8,128)S(1)} fusion(bf16[96,4096]{1,0:T(8,128)(2,1)S(1)} %copy-done.5, bf16[4096,4096]{1,0:T(8,128)(2,1)} %param.10), kind=kOutput, calls=%fused_computation.147 | convolution fusion | flops 3221225472 | bytes 35913728 | tf_op jit(solution)/shard_map/dot_general | solution.py:201
  21.3 0.9 fusion.31
  22.2 1.4 fusion.25
  23.6 1.0 pad_maximum_fusion
  26.6 13.6 %fusion.43 = f32[96,4096]{1,0:T(8,128)S(1)} fusion(bf16[96,4096]{1,0:T(8,128)(2,1)} %collective-permute-done.1, bf16[4096,4096]{1,0:T(8,128)(2,1)} %param.10), kind=kOutput, calls=%fused_computation.150 | convolution fusion | flops 3221225472 | bytes 35913728 | tf_op jit(solution)/shard_map/dot_general | solution.py:201
  40.2 0.7 collective-permute-start.4
  40.9 1.6 fusion.44
  42.6 1.7 fusion.45
  44.4 2.2 broadcast_select_fusion.3
  46.6 1.5 collective-permute-start.2
  48.4 1.0 pad_maximum_fusion.1
  49.4 10.9 %collective-permute-done.4 = bf16[96,4096]{1,0:T(8,128)(2,1)S(1)} collective-permute-done((bf16[96,4096]{1,0:T(8,128)(2,1)}, bf16[96,4096]{1,0:T(8,128)(2,1)S(1)}, u32[]{:S(2)}, u32[]{:S(2)}) %collective-permute-start.4) | collective-permute-done | bytes 786464 | tf_op jit(solution)/shard_map/ppermute | solution.py:200
  60.3 13.4 %fusion.46 = f32[96,4096]{1,0:T(8,128)S(1)} fusion(bf16[96,4096]{1,0:T(8,128)(2,1)S(1)} %collective-permute-done.4, bf16[4096,4096]{1,0:T(8,128)(2,1)} %param.10), kind=kOutput, calls=%fused_computation.153 | convolution fusion | flops 3221225472 | bytes 35913728 | tf_op jit(solution)/shard_map/dot_general | solution.py:201
  73.7 2.7 %collective-permute-start.7 = (bf16[96,4096]{1,0:T(8,128)(2,1)S(1)}, bf16[96,4096]{1,0:T(8,128)(2,1)S(1)}, u32[]{:S(2)}, u32[]{:S(2)}) collective-permute-start(bf16[96,4096]{1,0:T(8,128)(2,1)S(1)} %collective-permute-done.4), channel_id=1, source_target_pairs={{0,3},{1,0},{2,1},{3,2},{4,7},{5,4},{6,5},{7,6},{8,11},{9,8},{10,9... | collective-permute-start | bytes 2359304 | tf_op jit(solution)/shard_map/ppermute | solution.py:200
  77.4 1.1 broadcast_select_fusion.2
  78.5 1.5 collective-permute-start.5
  80.4 1.0 pad_maximum_fusion.2
  82.5 1.6 select_add_fusion.3
  84.3 8.6 %collective-permute-done.7 = bf16[96,4096]{1,0:T(8,128)(2,1)S(1)} collective-permute-done((bf16[96,4096]{1,0:T(8,128)(2,1)S(1)}, bf16[96,4096]{1,0:T(8,128)(2,1)S(1)}, u32[]{:S(2)}, u32[]{:S(2)}) %collective-permute-start.7) | collective-permute-done | bytes 786464 | tf_op jit(solution)/shard_map/ppermute | solution.py:200
  93.0 13.4 %fusion.49 = f32[96,4096]{1,0:T(8,128)S(1)} fusion(bf16[96,4096]{1,0:T(8,128)(2,1)S(1)} %collective-permute-done.7, bf16[4096,4096]{1,0:T(8,128)(2,1)} %param.10), kind=kOutput, calls=%fused_computation.156 | convolution fusion | flops 3221225472 | bytes 35913728 | tf_op jit(solution)/shard_map/dot_general | solution.py:201
  107.9 0.6 copy-done.9
  108.9 1.4 broadcast_select_fusion.1
  110.3 1.6 collective-permute-start.8
  111.9 1.3 select_add_fusion.2
  114.0 10.5 %collective-permute-done.8 = f32[96,1280]{1,0:T(8,128)S(1)} collective-permute-done((f32[96,1280]{1,0:T(8,128)S(1)}, f32[96,1280]{1,0:T(8,128)S(1)}, u32[]{:S(2)}, u32[]{:S(2)}) %collective-permute-start.8) | collective-permute-done | bytes 491552 | tf_op jit(solution)/shard_map/ppermute | solution.py:136
  124.5 1.4 select_add_fusion.1
  126.1 7.5 %collective-permute-done.10 = f32[96,1280]{1,0:T(8,128)S(1)} collective-permute-done((f32[96,1280]{1,0:T(8,128)S(1)}, f32[96,1280]{1,0:T(8,128)S(1)}, u32[]{:S(2)}, u32[]{:S(2)}) %collective-permute-start.10) | collective-permute-done | bytes 491552 | tf_op jit(solution)/shard_map/ppermute | solution.py:136
  133.9 11.5 %shard_map.91 = bf16[384,1024]{1,0:T(8,128)(2,1)S(1)} custom-call(f32[384,1024]{1,0:T(8,128)S(1)} %slice_dynamic-update-slice_fusion.query_ref, f32[384,256]{1,0:T(8,128)S(1)} %slice_dynamic-update-slice_fusion.4.pair_ref, f32[384,128]{1,0:T(8,128)S(1)} %copy.17.cos_ref, f32[384,128]{1,0:T(8,128)S(1)} %copy.18.sin_ref, s32[32,3]{1,0:T(8,128)S(1)} %copy.19.vert_ref, ...), custom_call_target="tpu_custom_call" | custom-call | tf_op jit(solution)/shard_map/pallas_call | solution.py:115
  145.5 1.6 collective-permute-start.14
  147.1 4.2 %collective-permute-done.14 = bf16[96,1024]{1,0:T(8,128)(2,1)S(1)} collective-permute-done((bf16[96,1024]{1,0:T(8,128)(2,1)S(1)}, bf16[96,1024]{1,0:T(8,128)(2,1)S(1)}, u32[]{:S(2)}, u32[]{:S(2)}) %collective-permute-start.14) | collective-permute-done | bytes 196640 | tf_op jit(solution)/shard_map/ppermute | solution.py:136
  151.4 1.6 collective-permute-start.11
  153.5 1.6 collective-permute-start.13
  155.1 7.5 %fusion.14 = bf16[96,2048]{1,0:T(8,128)(2,1)S(1)} fusion(bf16[4096,4096]{1,0:T(8,128)(2,1)} %param.13, bf16[96,1024]{1,0:T(8,128)(2,1)S(1)} %get-tuple-element.133, bf16[96,1024]{1,0:T(8,128)(2,1)S(1)} %get-tuple-element.134, bf16[96,1024]{1,0:T(8,128)(2,1)S(1)} %get-tuple-element.118, bf16[96,1024]{1,0:T(8,128)(2,1)S(1)} %get-tuple-element.117), kind=kOutput, calls=%fused_computation.14 | convolution fusion | flops 1613758464 | bytes 17956864 | tf_op jit(solution)/shard_map/dot_general | solution.py:258
  162.6 4.5 %collective-permute-done.13 = bf16[96,1024]{1,0:T(8,128)(2,1)S(1)} collective-permute-done((bf16[96,1024]{1,0:T(8,128)(2,1)S(1)}, bf16[96,1024]{1,0:T(8,128)(2,1)S(1)}, u32[]{:S(2)}, u32[]{:S(2)}) %collective-permute-start.13) | collective-permute-done | bytes 196640 | tf_op jit(solution)/shard_map/ppermute | solution.py:136
  167.3 7.3 %fusion.16 = bf16[96,2048]{1,0:T(8,128)(2,1)S(1)} fusion(bf16[96,4096]{1,0:T(8,128)(2,1)S(1)} %pad_maximum_fusion.4, bf16[4096,4096]{1,0:T(8,128)(2,1)} %param.13), kind=kOutput, calls=%fused_computation.16 | convolution fusion | flops 1610809344 | bytes 17956864 | tf_op jit(solution)/shard_map/dot_general | solution.py:258
  175.0 7.3 %fusion.12 = f32[96,2048]{1,0:T(8,128)S(1)} fusion(bf16[96,4096]{1,0:T(8,128)(2,1)S(1)} %pad_maximum_fusion.5, bf16[4096,4096]{1,0:T(8,128)(2,1)} %param.13), kind=kOutput, calls=%fused_computation.12 | convolution fusion | flops 1610612736 | bytes 18350080 | tf_op jit(solution)/shard_map/dot_general | solution.py:258
  182.9 5.9 %collective-permute-done.18 = bf16[96,2048]{1,0:T(8,128)(2,1)S(1)} collective-permute-done((bf16[96,2048]{1,0:T(8,128)(2,1)S(1)}, bf16[96,2048]{1,0:T(8,128)(2,1)S(1)}, u32[]{:S(2)}, u32[]{:S(2)}) %collective-permute-start.18) | collective-permute-done | bytes 393248 | tf_op jit(solution)/shard_map/ppermute | solution.py:276
  188.9 7.3 %fusion.4 = f32[96,2048]{1,0:T(8,128)S(1)} fusion(bf16[96,4096]{1,0:T(8,128)(2,1)S(1)} %pad_maximum_fusion.5, bf16[4096,4096]{1,0:T(8,128)(2,1)} %param.13), kind=kOutput, calls=%fused_computation.4 | convolution fusion | flops 1610612736 | bytes 18350080 | tf_op jit(solution)/shard_map/dot_general | solution.py:258
  196.6 6.1 %collective-permute-done.19 = bf16[96,2048]{1,0:T(8,128)(2,1)S(1)} collective-permute-done((bf16[96,2048]{1,0:T(8,128)(2,1)S(1)}, bf16[96,2048]{1,0:T(8,128)(2,1)S(1)}, u32[]{:S(2)}, u32[]{:S(2)}) %collective-permute-start.19) | collective-permute-done | bytes 393248 | tf_op jit(solution)/shard_map/ppermute | solution.py:276
  202.9 7.3 %fusion.10 = f32[96,2048]{1,0:T(8,128)S(1)} fusion(bf16[96,4096]{1,0:T(8,128)(2,1)S(1)} %pad_maximum_fusion.6, bf16[4096,4096]{1,0:T(8,128)(2,1)} %param.13), kind=kOutput, calls=%fused_computation.10 | convolution fusion | flops 1610612736 | bytes 18350080 | tf_op jit(solution)/shard_map/dot_general | solution.py:258
  210.5 7.3 %fusion.2 = f32[96,2048]{1,0:T(8,128)S(1)} fusion(bf16[96,4096]{1,0:T(8,128)(2,1)S(1)} %pad_maximum_fusion.6, bf16[4096,4096]{1,0:T(8,128)(2,1)} %param.13), kind=kOutput, calls=%fused_computation.2 | convolution fusion | flops 1610612736 | bytes 18350080 | tf_op jit(solution)/shard_map/dot_general | solution.py:258
  217.8 6.4 %collective-permute-done.22 = bf16[96,2048]{1,0:T(8,128)(2,1)S(1)} collective-permute-done((bf16[96,2048]{1,0:T(8,128)(2,1)S(1)}, bf16[96,2048]{1,0:T(8,128)(2,1)S(1)}, u32[]{:S(2)}, u32[]{:S(2)}) %collective-permute-start.22) | collective-permute-done | bytes 393248 | tf_op jit(solution)/shard_map/ppermute | solution.py:276
  224.4 7.3 %fusion.8 = f32[96,2048]{1,0:T(8,128)S(1)} fusion(bf16[96,4096]{1,0:T(8,128)(2,1)S(1)} %pad_maximum_fusion.7, bf16[4096,4096]{1,0:T(8,128)(2,1)} %param.13), kind=kOutput, calls=%fused_computation.8 | convolution fusion | flops 1610612736 | bytes 18350080 | tf_op jit(solution)/shard_map/dot_general | solution.py:258
  232.4 7.4 %fusion = f32[96,2048]{1,0:T(8,128)S(1)} fusion(bf16[96,4096]{1,0:T(8,128)(2,1)S(1)} %pad_maximum_fusion.7, bf16[4096,4096]{1,0:T(8,128)(2,1)} %param.13), kind=kOutput, calls=%fused_computation | convolution fusion | flops 1610612736 | bytes 18350080 | tf_op jit(solution)/shard_map/dot_general | solution.py:258
  239.8 5.1 %collective-permute-done.24 = bf16[96,2048]{1,0:T(8,128)(2,1)S(1)} collective-permute-done((bf16[96,2048]{1,0:T(8,128)(2,1)S(1)}, bf16[96,2048]{1,0:T(8,128)(2,1)S(1)}, u32[]{:S(2)}, u32[]{:S(2)}) %collective-permute-start.24) | collective-permute-done | bytes 393248 | tf_op jit(solution)/shard_map/ppermute | solution.py:276
  245.0 0.9 pad_maximum_fusion.8
  (182 shorter events, 12.0 us)
Async XLA Ops:
  0.0 7.4 %copy-start = (bf16[4096,256]{1,0:T(8,128)(2,1)S(1)}, bf16[4096,256]{1,0:T(8,128)(2,1)}, u32[]{:S(2)}) copy-start(bf16[4096,256]{1,0:T(8,128)(2,1)} %param.11) | copy-start | bytes 6291460
  0.0 7.4 %copy-start.5 = (bf16[96,4096]{1,0:T(8,128)(2,1)S(1)}, bf16[96,4096]{1,0:T(8,128)(2,1)}, u32[]{:S(2)}) copy-start(bf16[96,4096]{1,0:T(8,128)(2,1)} %param.9) | copy-start | bytes 2359300
  0.0 26.6 %collective-permute-start.1 = (bf16[96,4096]{1,0:T(8,128)(2,1)}, bf16[96,4096]{1,0:T(8,128)(2,1)}, u32[]{:S(2)}, u32[]{:S(2)}) collective-permute-start(bf16[96,4096]{1,0:T(8,128)(2,1)} %param.9), channel_id=1, source_target_pairs={{0,3},{1,0},{2,1},{3,2},{4,7},{5,4},{6,5},{7,6},{8,11},{9,8},{10,9... | collective-permute-start | bytes 2359304 | tf_op jit(solution)/shard_map/ppermute | solution.py:200
  7.4 14.8 %copy-start.31 = (f32[96,128]{1,0:T(8,128)}, f32[96,128]{1,0:T(8,128)S(1)}, u32[]{:S(2)}) copy-start(f32[96,128]{1,0:T(8,128)S(1)} %get-tuple-element.152) | copy-start | bytes 147460
  7.4 37.0 %copy-start.29 = (f32[96,128]{1,0:T(8,128)}, f32[96,128]{1,0:T(8,128)S(1)}, u32[]{:S(2)}) copy-start(f32[96,128]{1,0:T(8,128)S(1)} %get-tuple-element.151) | copy-start | bytes 147460
  7.9 14.3 %copy-start.34 = (f32[96,128]{1,0:T(8,128)}, f32[96,128]{1,0:T(8,128)S(1)}, u32[]{:S(2)}) copy-start(f32[96,128]{1,0:T(8,128)S(1)} %get-tuple-element.149) | copy-start | bytes 147460
  7.9 14.3 %copy-start.37 = (f32[96,128]{1,0:T(8,128)}, f32[96,128]{1,0:T(8,128)S(1)}, u32[]{:S(2)}) copy-start(f32[96,128]{1,0:T(8,128)S(1)} %get-tuple-element.150) | copy-start | bytes 147460
  22.2 2.5 %copy-start.20 = (f32[96,1024]{1,0:T(8,128)}, f32[96,1024]{1,0:T(8,128)S(1)}, u32[]{:S(2)}) copy-start(f32[96,1024]{1,0:T(8,128)S(1)} %get-tuple-element.99) | copy-start | bytes 1179652
  22.2 22.2 %copy-start.16 = (f32[96,1024]{1,0:T(8,128)}, f32[96,1024]{1,0:T(8,128)S(1)}, u32[]{:S(2)}) copy-start(f32[96,1024]{1,0:T(8,128)S(1)} %get-tuple-element.97) | copy-start | bytes 1179652
  22.2 22.2 %copy-start.18 = (f32[96,1024]{1,0:T(8,128)}, f32[96,1024]{1,0:T(8,128)S(1)}, u32[]{:S(2)}) copy-start(f32[96,1024]{1,0:T(8,128)S(1)} %get-tuple-element.98) | copy-start | bytes 1179652
  24.6 19.7 %collective-permute-start = (f32[96,2560]{1,0:T(8,128)}, f32[96,2560]{1,0:T(8,128)}, u32[]{:S(2)}, u32[]{:S(2)}) collective-permute-start(f32[96,2560]{1,0:T(8,128)} %pad_maximum_fusion), channel_id=1, source_target_pairs={{0,4},{4,0},{8,12},{12,8},{1,5},{5,1},{9,13},{13,9},{2,6},{6,2},{1... | collective-permute-start | bytes 2949128 | tf_op jit(solution)/shard_map/ppermute | solution.py:136
  40.2 2.4 copy-start.4
  40.2 20.1 %collective-permute-start.4 = (bf16[96,4096]{1,0:T(8,128)(2,1)}, bf16[96,4096]{1,0:T(8,128)(2,1)S(1)}, u32[]{:S(2)}, u32[]{:S(2)}) collective-permute-start(bf16[96,4096]{1,0:T(8,128)(2,1)} %collective-permute-done.1), channel_id=1, source_target_pairs={{0,3},{1,0},{2,1},{3,2},{4,7},{5,4},{6,5},{7,6},{8,11},{9,8},{10,9... | collective-permute-start | bytes 2359304 | tf_op jit(solution)/shard_map/ppermute | solution.py:200
  46.6 30.8 %collective-permute-start.2 = (f32[96,1280]{1,0:T(8,128)}, f32[96,1280]{1,0:T(8,128)}, u32[]{:S(2)}, u32[]{:S(2)}) collective-permute-start(f32[96,1280]{1,0:T(8,128)} %broadcast_select_fusion.3), channel_id=1, source_target_pairs={{0,8},{4,12},{8,0},{12,4},{1,9},{5,13},{9,1},{13,5},{2,10},{6,14},... | collective-permute-start | bytes 1474568 | tf_op jit(solution)/shard_map/ppermute | solution.py:136
  48.3 29.1 %copy-start.6 = (f32[96,1024]{1,0:T(8,128)}, f32[96,1024]{1,0:T(8,128)S(1)}, u32[]{:S(2)}) copy-start(f32[96,1024]{1,0:T(8,128)S(1)} %get-tuple-element.96) | copy-start | bytes 1179652
  49.4 27.9 %collective-permute-start.3 = (f32[96,2560]{1,0:T(8,128)}, f32[96,2560]{1,0:T(8,128)S(1)}, u32[]{:S(2)}, u32[]{:S(2)}) collective-permute-start(f32[96,2560]{1,0:T(8,128)} %pad_maximum_fusion.1), channel_id=1, source_target_pairs={{0,4},{4,0},{8,12},{12,8},{1,5},{5,1},{9,13},{13,9},{2,6},{6,2},{1... | collective-permute-start | bytes 2949128 | tf_op jit(solution)/shard_map/ppermute | solution.py:136
  73.7 19.3 %collective-permute-start.7 = (bf16[96,4096]{1,0:T(8,128)(2,1)S(1)}, bf16[96,4096]{1,0:T(8,128)(2,1)S(1)}, u32[]{:S(2)}, u32[]{:S(2)}) collective-permute-start(bf16[96,4096]{1,0:T(8,128)(2,1)S(1)} %collective-permute-done.4), channel_id=1, source_target_pairs={{0,3},{1,0},{2,1},{3,2},{4,7},{5,4},{6,5},{7,6},{8,11},{9,8},{10,9... | collective-permute-start | bytes 2359304 | tf_op jit(solution)/shard_map/ppermute | solution.py:200
  77.3 3.0 %copy-start.27 = (f32[96,128]{1,0:T(8,128)}, f32[96,128]{1,0:T(8,128)S(1)}, u32[]{:S(2)}) copy-start(f32[96,128]{1,0:T(8,128)S(1)} %get-tuple-element.160) | copy-start | bytes 147460
  78.5 28.9 %collective-permute-start.5 = (f32[96,1280]{1,0:T(8,128)}, f32[96,1280]{1,0:T(8,128)}, u32[]{:S(2)}, u32[]{:S(2)}) collective-permute-start(f32[96,1280]{1,0:T(8,128)} %broadcast_select_fusion.2), channel_id=1, source_target_pairs={{0,8},{4,12},{8,0},{12,4},{1,9},{5,13},{9,1},{13,5},{2,10},{6,14},... | collective-permute-start | bytes 1474568 | tf_op jit(solution)/shard_map/ppermute | solution.py:136
  80.2 2.1 copy-start.22
  80.2 2.2 copy-start.24
  80.2 2.2 copy-start.30
  80.2 2.2 copy-start.33
  80.3 2.2 copy-start.36
  80.3 2.2 copy-start.39
  81.6 25.7 %collective-permute-start.6 = (f32[96,2560]{1,0:T(8,128)}, f32[96,2560]{1,0:T(8,128)}, u32[]{:S(2)}, u32[]{:S(2)}) collective-permute-start(f32[96,2560]{1,0:T(8,128)} %pad_maximum_fusion.2), channel_id=1, source_target_pairs={{0,4},{4,0},{8,12},{12,8},{1,5},{5,1},{9,13},{13,9},{2,6},{6,2},{1... | collective-permute-start | bytes 2949128 | tf_op jit(solution)/shard_map/ppermute | solution.py:136
  107.8 4.1 %copy-start.7 = (f32[96,1024]{1,0:T(8,128)S(1)}, f32[96,1024]{1,0:T(8,128)}, u32[]{:S(2)}) copy-start(f32[96,1024]{1,0:T(8,128)} %copy-done.6) | copy-start | bytes 1179652
  107.8 4.1 %copy-start.26 = (f32[96,2560]{1,0:T(8,128)S(1)}, f32[96,2560]{1,0:T(8,128)}, u32[]{:S(2)}) copy-start(f32[96,2560]{1,0:T(8,128)} %copy-done.25) | copy-start | bytes 2949124
  107.8 5.4 %collective-permute-start.9 = (f32[96,2560]{1,0:T(8,128)S(1)}, f32[96,2560]{1,0:T(8,128)S(1)}, u32[]{:S(2)}, u32[]{:S(2)}) collective-permute-start(f32[96,2560]{1,0:T(8,128)S(1)} %pad_maximum_fusion.3), channel_id=1, source_target_pairs={{0,4},{4,0},{8,12},{12,8},{1,5},{5,1},{9,13},{13,9},{2,6},{6,2},{1... | collective-permute-start | bytes 2949128 | tf_op jit(solution)/shard_map/ppermute | solution.py:136
  110.3 14.2 %collective-permute-start.8 = (f32[96,1280]{1,0:T(8,128)S(1)}, f32[96,1280]{1,0:T(8,128)S(1)}, u32[]{:S(2)}, u32[]{:S(2)}) collective-permute-start(f32[96,1280]{1,0:T(8,128)S(1)} %broadcast_select_fusion.1), channel_id=1, source_target_pairs={{0,8},{4,12},{8,0},{12,4},{1,9},{5,13},{9,1},{13,5},{2,10},{6,14},... | collective-permute-start | bytes 1474568 | tf_op jit(solution)/shard_map/ppermute | solution.py:136
  113.5 20.1 %collective-permute-start.10 = (f32[96,1280]{1,0:T(8,128)S(1)}, f32[96,1280]{1,0:T(8,128)S(1)}, u32[]{:S(2)}, u32[]{:S(2)}) collective-permute-start(f32[96,1280]{1,0:T(8,128)S(1)} %broadcast_select_fusion), channel_id=1, source_target_pairs={{0,8},{4,12},{8,0},{12,4},{1,9},{5,13},{9,1},{13,5},{2,10},{6,14},... | collective-permute-start | bytes 1474568 | tf_op jit(solution)/shard_map/ppermute | solution.py:136
  126.0 7.8 %copy-start.2 = (s32[32]{0:T(128)S(1)}, s32[32]{0:T(128)}, u32[]{:S(2)}) copy-start(s32[32]{0:T(128)} %vert_live_ref.1) | copy-start | bytes 388
  126.1 7.8 %copy-start.3 = (s32[32]{0:T(128)S(1)}, s32[32]{0:T(128)}, u32[]{:S(2)}) copy-start(s32[32]{0:T(128)} %slash_live_ref.1) | copy-start | bytes 388
  145.5 5.7 %collective-permute-start.14 = (bf16[96,1024]{1,0:T(8,128)(2,1)S(1)}, bf16[96,1024]{1,0:T(8,128)(2,1)S(1)}, u32[]{:S(2)}, u32[]{:S(2)}) collective-permute-start(bf16[96,1024]{1,0:T(8,128)(2,1)S(1)} %get-tuple-element.101), channel_id=1, source_target_pairs={{0,8},{4,12},{8,0},{12,4},{1,9},{5,13},{9,1},{13,5},{2,10},{6,14},... | collective-permute-start | bytes 589832 | tf_op jit(solution)/shard_map/ppermute | solution.py:136
  151.3 3.7 %collective-permute-start.15 = (bf16[96,2048]{1,0:T(8,128)(2,1)S(1)}, bf16[96,2048]{1,0:T(8,128)(2,1)S(1)}, u32[]{:S(2)}, u32[]{:S(2)}) collective-permute-start(bf16[96,2048]{1,0:T(8,128)(2,1)S(1)} %pad_maximum_fusion.41), channel_id=1, source_target_pairs={{0,4},{4,0},{8,12},{12,8},{1,5},{5,1},{9,13},{13,9},{2,6},{6,2},{1... | collective-permute-start | bytes 1179656 | tf_op jit(solution)/shard_map/ppermute | solution.py:136
  151.4 58.8 %collective-permute-start.11 = (bf16[96,1024]{1,0:T(8,128)(2,1)S(1)}, bf16[96,1024]{1,0:T(8,128)(2,1)S(1)}, u32[]{:S(2)}, u32[]{:S(2)}) collective-permute-start(bf16[96,1024]{1,0:T(8,128)(2,1)S(1)} %get-tuple-element.104), channel_id=1, source_target_pairs={{0,8},{4,12},{8,0},{12,4},{1,9},{5,13},{9,1},{13,5},{2,10},{6,14},... | collective-permute-start | bytes 589832 | tf_op jit(solution)/shard_map/ppermute | solution.py:136
  152.9 29.3 %collective-permute-start.12 = (bf16[96,1024]{1,0:T(8,128)(2,1)S(1)}, bf16[96,1024]{1,0:T(8,128)(2,1)S(1)}, u32[]{:S(2)}, u32[]{:S(2)}) collective-permute-start(bf16[96,1024]{1,0:T(8,128)(2,1)S(1)} %get-tuple-element.103), channel_id=1, source_target_pairs={{0,8},{4,12},{8,0},{12,4},{1,9},{5,13},{9,1},{13,5},{2,10},{6,14},... | collective-permute-start | bytes 589832 | tf_op jit(solution)/shard_map/ppermute | solution.py:136
  153.5 13.7 %collective-permute-start.13 = (bf16[96,1024]{1,0:T(8,128)(2,1)S(1)}, bf16[96,1024]{1,0:T(8,128)(2,1)S(1)}, u32[]{:S(2)}, u32[]{:S(2)}) collective-permute-start(bf16[96,1024]{1,0:T(8,128)(2,1)S(1)} %get-tuple-element.102), channel_id=1, source_target_pairs={{0,8},{4,12},{8,0},{12,4},{1,9},{5,13},{9,1},{13,5},{2,10},{6,14},... | collective-permute-start | bytes 589832 | tf_op jit(solution)/shard_map/ppermute | solution.py:136
  167.2 7.7 %collective-permute-start.16 = (bf16[96,2048]{1,0:T(8,128)(2,1)S(1)}, bf16[96,2048]{1,0:T(8,128)(2,1)S(1)}, u32[]{:S(2)}, u32[]{:S(2)}) collective-permute-start(bf16[96,2048]{1,0:T(8,128)(2,1)S(1)} %pad_maximum_fusion.42), channel_id=1, source_target_pairs={{0,4},{4,0},{8,12},{12,8},{1,5},{5,1},{9,13},{13,9},{2,6},{6,2},{1... | collective-permute-start | bytes 1179656 | tf_op jit(solution)/shard_map/ppermute | solution.py:136
  174.6 14.2 %collective-permute-start.18 = (bf16[96,2048]{1,0:T(8,128)(2,1)S(1)}, bf16[96,2048]{1,0:T(8,128)(2,1)S(1)}, u32[]{:S(2)}, u32[]{:S(2)}) collective-permute-start(bf16[96,2048]{1,0:T(8,128)(2,1)S(1)} %fusion.14), channel_id=1, source_target_pairs={{0,1},{1,2},{2,3},{3,0},{4,5},{5,6},{6,7},{7,4},{8,9},{9,10},{10,1... | collective-permute-start | bytes 1179656 | tf_op jit(solution)/shard_map/ppermute | solution.py:276
  182.3 20.4 %collective-permute-start.17 = (bf16[96,2048]{1,0:T(8,128)(2,1)S(1)}, bf16[96,2048]{1,0:T(8,128)(2,1)S(1)}, u32[]{:S(2)}, u32[]{:S(2)}) collective-permute-start(bf16[96,2048]{1,0:T(8,128)(2,1)S(1)} %pad_maximum_fusion.43), channel_id=1, source_target_pairs={{0,4},{4,0},{8,12},{12,8},{1,5},{5,1},{9,13},{13,9},{2,6},{6,2},{1... | collective-permute-start | bytes 1179656 | tf_op jit(solution)/shard_map/ppermute | solution.py:136
  188.8 13.8 %collective-permute-start.19 = (bf16[96,2048]{1,0:T(8,128)(2,1)S(1)}, bf16[96,2048]{1,0:T(8,128)(2,1)S(1)}, u32[]{:S(2)}, u32[]{:S(2)}) collective-permute-start(bf16[96,2048]{1,0:T(8,128)(2,1)S(1)} %fusion.16), channel_id=1, source_target_pairs={{0,1},{1,2},{2,3},{3,0},{4,5},{5,6},{6,7},{7,4},{8,9},{9,10},{10,1... | collective-permute-start | bytes 1179656 | tf_op jit(solution)/shard_map/ppermute | solution.py:276
  196.2 14.2 %collective-permute-start.21 = (bf16[96,2048]{1,0:T(8,128)(2,1)S(1)}, bf16[96,2048]{1,0:T(8,128)(2,1)S(1)}, u32[]{:S(2)}, u32[]{:S(2)}) collective-permute-start(bf16[96,2048]{1,0:T(8,128)(2,1)S(1)} %add_convert_fusion.5), channel_id=1, source_target_pairs={{0,1},{1,2},{2,3},{3,0},{4,5},{5,6},{6,7},{7,4},{8,9},{9,10},{10,1... | collective-permute-start | bytes 1179656 | tf_op jit(solution)/shard_map/ppermute | solution.py:276
  210.3 14.0 %collective-permute-start.20 = (bf16[96,2048]{1,0:T(8,128)(2,1)S(1)}, bf16[96,2048]{1,0:T(8,128)(2,1)S(1)}, u32[]{:S(2)}, u32[]{:S(2)}) collective-permute-start(bf16[96,2048]{1,0:T(8,128)(2,1)S(1)} %pad_maximum_fusion.44), channel_id=1, source_target_pairs={{0,4},{4,0},{8,12},{12,8},{1,5},{5,1},{9,13},{13,9},{2,6},{6,2},{1... | collective-permute-start | bytes 1179656 | tf_op jit(solution)/shard_map/ppermute | solution.py:136
  210.4 13.8 %collective-permute-start.22 = (bf16[96,2048]{1,0:T(8,128)(2,1)S(1)}, bf16[96,2048]{1,0:T(8,128)(2,1)S(1)}, u32[]{:S(2)}, u32[]{:S(2)}) collective-permute-start(bf16[96,2048]{1,0:T(8,128)(2,1)S(1)} %add_convert_fusion.4), channel_id=1, source_target_pairs={{0,1},{1,2},{2,3},{3,0},{4,5},{5,6},{6,7},{7,4},{8,9},{9,10},{10,1... | collective-permute-start | bytes 1179656 | tf_op jit(solution)/shard_map/ppermute | solution.py:276
  217.8 14.4 %collective-permute-start.23 = (bf16[96,2048]{1,0:T(8,128)(2,1)S(1)}, bf16[96,2048]{1,0:T(8,128)(2,1)S(1)}, u32[]{:S(2)}, u32[]{:S(2)}) collective-permute-start(bf16[96,2048]{1,0:T(8,128)(2,1)S(1)} %add_convert_fusion.3), channel_id=1, source_target_pairs={{0,1},{1,2},{2,3},{3,0},{4,5},{5,6},{6,7},{7,4},{8,9},{9,10},{10,1... | collective-permute-start | bytes 1179656 | tf_op jit(solution)/shard_map/ppermute | solution.py:276
  232.3 12.6 %collective-permute-start.24 = (bf16[96,2048]{1,0:T(8,128)(2,1)S(1)}, bf16[96,2048]{1,0:T(8,128)(2,1)S(1)}, u32[]{:S(2)}, u32[]{:S(2)}) collective-permute-start(bf16[96,2048]{1,0:T(8,128)(2,1)S(1)} %add_convert_fusion.2), channel_id=1, source_target_pairs={{0,1},{1,2},{2,3},{3,0},{4,5},{5,6},{6,7},{7,4},{8,9},{9,10},{10,1... | collective-permute-start | bytes 1179656 | tf_op jit(solution)/shard_map/ppermute | solution.py:276
  232.4 13.5 %copy-start.1 = (bf16[4096,256]{1,0:T(8,128)(2,1)S(1)}, bf16[4096,256]{1,0:T(8,128)(2,1)}, u32[]{:S(2)}) copy-start(bf16[4096,256]{1,0:T(8,128)(2,1)} %param.11) | copy-start | bytes 6291460
  (19 other events, 28.3 us)

commit v3 on v2

--- a/solution.py
+++ b/solution.py
@@ -255,13 +255,17 @@
     for step in range(ring):
         terms = []
         for part in range(PARTS):
+            if step > 0:
+                gathered, got[part] = lax.optimization_barrier((gathered, got[part]))
             term = jnp.dot(
                 gathered,
                 w_out[:, part * columns : (part + 1) * columns],
                 preferred_element_type=jnp.float32,
             )
             if part == 0 and step + 1 < ring:
-                landed, term = lax.optimization_barrier((halfway[step + 1], term))
+                landed = halfway[step + 1]
+                if step > 0:
+                    landed, term = lax.optimization_barrier((landed, term))
                 following = gather_rest(pieces[step + 1], landed, seq_size, seq_rank)
             if step > 0:
                 term, arrived = lax.optimization_barrier((term, got[part]))

time: 246 us -> 279 us (1.13)
  waiting for transfers between devices: 70.1 us -> 103 us
    ppermute x6, waiting for transfers between devices: 23.9 us -> 51.6 us  [on_device(): got[part] = lax.ppermute(term, 'tp', up)]
    ppermute x16, waiting for transfers between devices: 26.7 us -> 31.9 us  [swap_with(): lax.ppermute(value, 'seq', [(rank, rank ^ bit) for rank in range(size)])]
  transfers between devices with their start and end apart: 25 -> 25, of which waited for: 11 -> 12; matrix products, arithmetic and copies ran while one was open for 56% -> 44% of each run, Pallas kernels for 0% -> 0%
where the time goes in v3:
time: 279 us; the launch traced here: 278 us
  matrix products  120 us (43%)
  waiting for transfers between devices  103 us (37%)
  starting transfers between devices  20.4 us (7%)
  other arithmetic  17.3 us (6%)
  Pallas kernels  11.5 us (4%)
  local copies, waits for them, and re-layouts  4.88 us (2%)
    dot_general x8, matrix products, on_device(): jnp.dot(gathered, w_out[:, part * columns:(part + 1) * columns], preferre...  58.5 us
    dot_general x4, matrix products, on_device(): query = jnp.dot(held, w_query, preferred_element_type=jnp.float32)  53.7 us
    ppermute x6, waiting for transfers between devices, on_device(): got[part] = lax.ppermute(term, 'tp', up)  51.6 us
    ppermute x16, waiting for transfers between devices, swap_with(): lax.ppermute(value, 'seq', [(rank, rank ^ bit) for rank in range(size)])  31.9 us
    ppermute x3, waiting for transfers between devices, on_device(): later = lax.ppermute(held, 'tp', down) if step < ring - 1 else None  19.5 us
    pallas_call x1, Pallas kernels, attend(): pl.pallas_call(functools.partial(attend_kernel, heads_here), grid=(heads_...  11.5 us
    ppermute x16, starting transfers between devices, swap_with(): lax.ppermute(value, 'seq', [(rank, rank ^ bit) for rank in range(size)])  9.68 us
    ppermute x3, starting transfers between devices, on_device(): later = lax.ppermute(held, 'tp', down) if step < ring - 1 else None  8.47 us
  transfers between devices with their start and end apart: 25, of which 12 were waited for; matrix products, arithmetic and copies ran while one was open for 44% of the time, Pallas kernels for 0%

profile of v3, /device:TPU:0, one launch (start us, length us, event | category | flops | bytes accessed | tf_op | source)
XLA Modules:
  0.0 278.5 jit_solution(12731498212356814742)
XLA Ops:
  0.0 5.0 %collective-permute-start.1 = (bf16[96,4096]{1,0:T(8,128)(2,1)}, bf16[96,4096]{1,0:T(8,128)(2,1)}, u32[]{:S(2)}, u32[]{:S(2)}) collective-permute-start(bf16[96,4096]{1,0:T(8,128)(2,1)} %param.9), channel_id=1, source_target_pairs={{0,3},{1,0},{2,1},{3,2},{4,7},{5,4},{6,5},{7,6},{8,11},{9,8},{10,9... | collective-permute-start | bytes 2359304 | tf_op jit(solution)/shard_map/ppermute | solution.py:200
  5.1 2.3 fusion.45
  7.9 13.4 %fusion.43 = f32[96,4096]{1,0:T(8,128)S(1)} fusion(bf16[96,4096]{1,0:T(8,128)(2,1)S(1)} %copy-done.5, bf16[4096,4096]{1,0:T(8,128)(2,1)} %param.10), kind=kOutput, calls=%fused_computation.148 | convolution fusion | flops 3221225472 | bytes 35913728 | tf_op jit(solution)/shard_map/dot_general | solution.py:201
  21.3 0.9 fusion.34
  22.2 1.4 fusion.28
  23.6 1.0 pad_maximum_fusion
  26.6 13.6 %fusion.46 = f32[96,4096]{1,0:T(8,128)S(1)} fusion(bf16[96,4096]{1,0:T(8,128)(2,1)} %collective-permute-done.1, bf16[4096,4096]{1,0:T(8,128)(2,1)} %param.10), kind=kOutput, calls=%fused_computation.151 | convolution fusion | flops 3221225472 | bytes 35913728 | tf_op jit(solution)/shard_map/dot_general | solution.py:201
  40.2 0.7 collective-permute-start.4
  40.9 1.6 fusion.47
  42.6 1.7 fusion.48
  44.4 2.2 broadcast_select_fusion.3
  46.6 1.5 collective-permute-start.2
  48.4 1.0 pad_maximum_fusion.1
  49.4 10.9 %collective-permute-done.4 = bf16[96,4096]{1,0:T(8,128)(2,1)S(1)} collective-permute-done((bf16[96,4096]{1,0:T(8,128)(2,1)}, bf16[96,4096]{1,0:T(8,128)(2,1)S(1)}, u32[]{:S(2)}, u32[]{:S(2)}) %collective-permute-start.4) | collective-permute-done | bytes 786464 | tf_op jit(solution)/shard_map/ppermute | solution.py:200
  60.3 13.4 %fusion.49 = f32[96,4096]{1,0:T(8,128)S(1)} fusion(bf16[96,4096]{1,0:T(8,128)(2,1)S(1)} %collective-permute-done.4, bf16[4096,4096]{1,0:T(8,128)(2,1)} %param.10), kind=kOutput, calls=%fused_computation.154 | convolution fusion | flops 3221225472 | bytes 35913728 | tf_op jit(solution)/shard_map/dot_general | solution.py:201
  73.7 2.7 collective-permute-start.7
  77.4 1.1 broadcast_select_fusion.2
  78.5 1.5 collective-permute-start.5
  80.4 1.0 pad_maximum_fusion.2
  82.5 1.6 select_add_fusion.3
  84.3 8.6 %collective-permute-done.7 = bf16[96,4096]{1,0:T(8,128)(2,1)S(1)} collective-permute-done((bf16[96,4096]{1,0:T(8,128)(2,1)S(1)}, bf16[96,4096]{1,0:T(8,128)(2,1)S(1)}, u32[]{:S(2)}, u32[]{:S(2)}) %collective-permute-start.7) | collective-permute-done | bytes 786464 | tf_op jit(solution)/shard_map/ppermute | solution.py:200
  93.0 13.4 %fusion.52 = f32[96,4096]{1,0:T(8,128)S(1)} fusion(bf16[96,4096]{1,0:T(8,128)(2,1)S(1)} %collective-permute-done.7, bf16[4096,4096]{1,0:T(8,128)(2,1)} %param.10), kind=kOutput, calls=%fused_computation.157 | convolution fusion | flops 3221225472 | bytes 35913728 | tf_op jit(solution)/shard_map/dot_general | solution.py:201
  108.9 1.4 broadcast_select_fusion.1
  110.3 1.6 collective-permute-start.8
  111.9 1.3 select_add_fusion.2
  114.0 10.5 %collective-permute-done.8 = f32[96,1280]{1,0:T(8,128)S(1)} collective-permute-done((f32[96,1280]{1,0:T(8,128)S(1)}, f32[96,1280]{1,0:T(8,128)S(1)}, u32[]{:S(2)}, u32[]{:S(2)}) %collective-permute-start.8) | collective-permute-done | bytes 491552 | tf_op jit(solution)/shard_map/ppermute | solution.py:136
  124.5 1.4 select_add_fusion.1
  126.1 7.5 %collective-permute-done.10 = f32[96,1280]{1,0:T(8,128)S(1)} collective-permute-done((f32[96,1280]{1,0:T(8,128)S(1)}, f32[96,1280]{1,0:T(8,128)S(1)}, u32[]{:S(2)}, u32[]{:S(2)}) %collective-permute-start.10) | collective-permute-done | bytes 491552 | tf_op jit(solution)/shard_map/ppermute | solution.py:136
  133.9 11.5 %shard_map.91 = bf16[384,1024]{1,0:T(8,128)(2,1)S(1)} custom-call(f32[384,1024]{1,0:T(8,128)S(1)} %slice_dynamic-update-slice_fusion.query_ref, f32[384,256]{1,0:T(8,128)S(1)} %slice_dynamic-update-slice_fusion.4.pair_ref, f32[384,128]{1,0:T(8,128)S(1)} %copy.17.cos_ref, f32[384,128]{1,0:T(8,128)S(1)} %copy.18.sin_ref, s32[32,3]{1,0:T(8,128)S(1)} %copy.19.vert_ref, ...), custom_call_target="tpu_custom_call" | custom-call | tf_op jit(solution)/shard_map/pallas_call | solution.py:115
  145.5 1.6 collective-permute-start.15
  147.6 1.5 collective-permute-start.12
  149.6 3.8 %collective-permute-done.15 = bf16[96,1024]{1,0:T(8,128)(2,1)S(1)} collective-permute-done((bf16[96,1024]{1,0:T(8,128)(2,1)S(1)}, bf16[96,1024]{1,0:T(8,128)(2,1)S(1)}, u32[]{:S(2)}, u32[]{:S(2)}) %collective-permute-start.15) | collective-permute-done | bytes 196640 | tf_op jit(solution)/shard_map/ppermute | solution.py:136
  153.5 10.1 %collective-permute-done.13 = bf16[96,1024]{1,0:T(8,128)(2,1)S(1)} collective-permute-done((bf16[96,1024]{1,0:T(8,128)(2,1)S(1)}, bf16[96,1024]{1,0:T(8,128)(2,1)S(1)}, u32[]{:S(2)}, u32[]{:S(2)}) %collective-permute-start.13) | collective-permute-done | bytes 196640 | tf_op jit(solution)/shard_map/ppermute | solution.py:136
  163.9 7.5 %fusion.16 = bf16[96,2048]{1,0:T(8,128)(2,1)S(1)} fusion(bf16[4096,4096]{1,0:T(8,128)(2,1)} %param.13, bf16[96,1024]{1,0:T(8,128)(2,1)S(1)} %get-tuple-element.149, bf16[96,1024]{1,0:T(8,128)(2,1)S(1)} %get-tuple-element.150, bf16[96,1024]{1,0:T(8,128)(2,1)S(1)} %get-tuple-element.134, bf16[96,1024]{1,0:T(8,128)(2,1)S(1)} %get-tuple-element.133), kind=kOutput, calls=%fused_computation.16 | convolution fusion | flops 1613955072 | bytes 17956864 | tf_op jit(solution)/shard_map/dot_general | solution.py:260
  171.3 7.3 %fusion.19 = bf16[96,2048]{1,0:T(8,128)(2,1)S(1)} fusion(bf16[96,4096]{1,0:T(8,128)(2,1)S(1)} %pad_maximum_fusion.5, bf16[4096,4096]{1,0:T(8,128)(2,1)} %param.13), kind=kOutput, calls=%fused_computation.17 | convolution fusion | flops 1610809344 | bytes 17956864 | tf_op jit(solution)/shard_map/dot_general | solution.py:260
  178.8 2.0 collective-permute-start.19
  180.8 12.0 %collective-permute-done.17 = bf16[96,2048]{1,0:T(8,128)(2,1)S(1)} collective-permute-done((bf16[96,2048]{1,0:T(8,128)(2,1)S(1)}, bf16[96,2048]{1,0:T(8,128)(2,1)S(1)}, u32[]{:S(2)}, u32[]{:S(2)}) %collective-permute-start.17) | collective-permute-done | bytes 393248 | tf_op jit(solution)/shard_map/ppermute | solution.py:280
  192.8 7.3 %fusion.12 = f32[96,2048]{1,0:T(8,128)S(1)} fusion(bf16[96,4096]{1,0:T(8,128)(2,1)S(1)} %pad_maximum_fusion.4, bf16[4096,4096]{1,0:T(8,128)(2,1)} %param.13), kind=kOutput, calls=%fused_computation.12 | convolution fusion | flops 1610612736 | bytes 18350080 | tf_op jit(solution)/shard_map/dot_general | solution.py:260
  200.3 0.7 collective-permute-done.19
  201.0 7.3 %fusion.4 = f32[96,2048]{1,0:T(8,128)S(1)} fusion(bf16[96,4096]{1,0:T(8,128)(2,1)S(1)} %pad_maximum_fusion.4, bf16[4096,4096]{1,0:T(8,128)(2,1)} %param.13), kind=kOutput, calls=%fused_computation.4 | convolution fusion | flops 1610612736 | bytes 18350080 | tf_op jit(solution)/shard_map/dot_general | solution.py:260
  208.6 12.5 %collective-permute-done.20 = bf16[96,2048]{1,0:T(8,128)(2,1)S(1)} collective-permute-done((bf16[96,2048]{1,0:T(8,128)(2,1)S(1)}, bf16[96,2048]{1,0:T(8,128)(2,1)S(1)}, u32[]{:S(2)}, u32[]{:S(2)}) %collective-permute-start.20) | collective-permute-done | bytes 393248 | tf_op jit(solution)/shard_map/ppermute | solution.py:280
  221.1 7.3 %fusion.10 = f32[96,2048]{1,0:T(8,128)S(1)} fusion(bf16[96,4096]{1,0:T(8,128)(2,1)S(1)} %pad_maximum_fusion.6, bf16[4096,4096]{1,0:T(8,128)(2,1)} %param.13), kind=kOutput, calls=%fused_computation.10 | convolution fusion | flops 1610612736 | bytes 18350080 | tf_op jit(solution)/shard_map/dot_general | solution.py:260
  228.7 13.5 %collective-permute-done.22 = bf16[96,2048]{1,0:T(8,128)(2,1)S(1)} collective-permute-done((bf16[96,2048]{1,0:T(8,128)(2,1)S(1)}, bf16[96,2048]{1,0:T(8,128)(2,1)S(1)}, u32[]{:S(2)}, u32[]{:S(2)}) %collective-permute-start.22) | collective-permute-done | bytes 393248 | tf_op jit(solution)/shard_map/ppermute | solution.py:280
  242.3 7.3 %fusion.2 = f32[96,2048]{1,0:T(8,128)S(1)} fusion(bf16[96,4096]{1,0:T(8,128)(2,1)S(1)} %pad_maximum_fusion.6, bf16[4096,4096]{1,0:T(8,128)(2,1)} %param.13), kind=kOutput, calls=%fused_computation.2 | convolution fusion | flops 1610612736 | bytes 18350080 | tf_op jit(solution)/shard_map/dot_general | solution.py:260
  250.2 7.3 %fusion.8 = f32[96,2048]{1,0:T(8,128)S(1)} fusion(bf16[96,4096]{1,0:T(8,128)(2,1)S(1)} %pad_maximum_fusion.7, bf16[4096,4096]{1,0:T(8,128)(2,1)} %param.13), kind=kOutput, calls=%fused_computation.8 | convolution fusion | flops 1610612736 | bytes 18350080 | tf_op jit(solution)/shard_map/dot_general | solution.py:260
  257.7 12.4 %collective-permute-done.24 = bf16[96,2048]{1,0:T(8,128)(2,1)S(1)} collective-permute-done((bf16[96,2048]{1,0:T(8,128)(2,1)S(1)}, bf16[96,2048]{1,0:T(8,128)(2,1)S(1)}, u32[]{:S(2)}, u32[]{:S(2)}) %collective-permute-start.24) | collective-permute-done | bytes 393248 | tf_op jit(solution)/shard_map/ppermute | solution.py:280
  270.0 7.4 %fusion = f32[96,2048]{1,0:T(8,128)S(1)} fusion(bf16[96,4096]{1,0:T(8,128)(2,1)S(1)} %pad_maximum_fusion.7, bf16[4096,4096]{1,0:T(8,128)(2,1)} %param.13), kind=kOutput, calls=%fused_computation | convolution fusion | flops 1610612736 | bytes 18350080 | tf_op jit(solution)/shard_map/dot_general | solution.py:260
  277.6 0.9 pad_maximum_fusion.8
  (182 shorter events, 12.0 us)
Async XLA Ops:
  0.0 7.4 %copy-start = (bf16[4096,256]{1,0:T(8,128)(2,1)S(1)}, bf16[4096,256]{1,0:T(8,128)(2,1)}, u32[]{:S(2)}) copy-start(bf16[4096,256]{1,0:T(8,128)(2,1)} %param.11) | copy-start | bytes 6291460
  0.0 7.4 %copy-start.5 = (bf16[96,4096]{1,0:T(8,128)(2,1)S(1)}, bf16[96,4096]{1,0:T(8,128)(2,1)}, u32[]{:S(2)}) copy-start(bf16[96,4096]{1,0:T(8,128)(2,1)} %param.9) | copy-start | bytes 2359300
  0.0 26.6 %collective-permute-start.1 = (bf16[96,4096]{1,0:T(8,128)(2,1)}, bf16[96,4096]{1,0:T(8,128)(2,1)}, u32[]{:S(2)}, u32[]{:S(2)}) collective-permute-start(bf16[96,4096]{1,0:T(8,128)(2,1)} %param.9), channel_id=1, source_target_pairs={{0,3},{1,0},{2,1},{3,2},{4,7},{5,4},{6,5},{7,6},{8,11},{9,8},{10,9... | collective-permute-start | bytes 2359304 | tf_op jit(solution)/shard_map/ppermute | solution.py:200
  7.4 14.8 %copy-start.31 = (f32[96,128]{1,0:T(8,128)}, f32[96,128]{1,0:T(8,128)S(1)}, u32[]{:S(2)}) copy-start(f32[96,128]{1,0:T(8,128)S(1)} %get-tuple-element.172) | copy-start | bytes 147460
  7.4 37.0 %copy-start.29 = (f32[96,128]{1,0:T(8,128)}, f32[96,128]{1,0:T(8,128)S(1)}, u32[]{:S(2)}) copy-start(f32[96,128]{1,0:T(8,128)S(1)} %get-tuple-element.171) | copy-start | bytes 147460
  7.9 14.3 %copy-start.34 = (f32[96,128]{1,0:T(8,128)}, f32[96,128]{1,0:T(8,128)S(1)}, u32[]{:S(2)}) copy-start(f32[96,128]{1,0:T(8,128)S(1)} %get-tuple-element.169) | copy-start | bytes 147460
  7.9 14.3 %copy-start.37 = (f32[96,128]{1,0:T(8,128)}, f32[96,128]{1,0:T(8,128)S(1)}, u32[]{:S(2)}) copy-start(f32[96,128]{1,0:T(8,128)S(1)} %get-tuple-element.170) | copy-start | bytes 147460
  22.2 2.5 copy-start.20
  22.2 22.2 %copy-start.16 = (f32[96,1024]{1,0:T(8,128)}, f32[96,1024]{1,0:T(8,128)S(1)}, u32[]{:S(2)}) copy-start(f32[96,1024]{1,0:T(8,128)S(1)} %get-tuple-element.117) | copy-start | bytes 1179652
  22.2 22.2 %copy-start.18 = (f32[96,1024]{1,0:T(8,128)}, f32[96,1024]{1,0:T(8,128)S(1)}, u32[]{:S(2)}) copy-start(f32[96,1024]{1,0:T(8,128)S(1)} %get-tuple-element.118) | copy-start | bytes 1179652
  24.6 19.7 %collective-permute-start = (f32[96,2560]{1,0:T(8,128)}, f32[96,2560]{1,0:T(8,128)}, u32[]{:S(2)}, u32[]{:S(2)}) collective-permute-start(f32[96,2560]{1,0:T(8,128)} %pad_maximum_fusion), channel_id=1, source_target_pairs={{0,4},{4,0},{8,12},{12,8},{1,5},{5,1},{9,13},{13,9},{2,6},{6,2},{1... | collective-permute-start | bytes 2949128 | tf_op jit(solution)/shard_map/ppermute | solution.py:136
  40.2 2.4 copy-start.4
  40.2 20.1 %collective-permute-start.4 = (bf16[96,4096]{1,0:T(8,128)(2,1)}, bf16[96,4096]{1,0:T(8,128)(2,1)S(1)}, u32[]{:S(2)}, u32[]{:S(2)}) collective-permute-start(bf16[96,4096]{1,0:T(8,128)(2,1)} %collective-permute-done.1), channel_id=1, source_target_pairs={{0,3},{1,0},{2,1},{3,2},{4,7},{5,4},{6,5},{7,6},{8,11},{9,8},{10,9... | collective-permute-start | bytes 2359304 | tf_op jit(solution)/shard_map/ppermute | solution.py:200
  46.6 30.8 %collective-permute-start.2 = (f32[96,1280]{1,0:T(8,128)}, f32[96,1280]{1,0:T(8,128)}, u32[]{:S(2)}, u32[]{:S(2)}) collective-permute-start(f32[96,1280]{1,0:T(8,128)} %broadcast_select_fusion.3), channel_id=1, source_target_pairs={{0,8},{4,12},{8,0},{12,4},{1,9},{5,13},{9,1},{13,5},{2,10},{6,14},... | collective-permute-start | bytes 1474568 | tf_op jit(solution)/shard_map/ppermute | solution.py:136
  48.3 29.1 %copy-start.6 = (f32[96,1024]{1,0:T(8,128)}, f32[96,1024]{1,0:T(8,128)S(1)}, u32[]{:S(2)}) copy-start(f32[96,1024]{1,0:T(8,128)S(1)} %get-tuple-element.116) | copy-start | bytes 1179652
  49.4 27.9 %collective-permute-start.3 = (f32[96,2560]{1,0:T(8,128)}, f32[96,2560]{1,0:T(8,128)S(1)}, u32[]{:S(2)}, u32[]{:S(2)}) collective-permute-start(f32[96,2560]{1,0:T(8,128)} %pad_maximum_fusion.1), channel_id=1, source_target_pairs={{0,4},{4,0},{8,12},{12,8},{1,5},{5,1},{9,13},{13,9},{2,6},{6,2},{1... | collective-permute-start | bytes 2949128 | tf_op jit(solution)/shard_map/ppermute | solution.py:136
  73.7 19.3 %collective-permute-start.7 = (bf16[96,4096]{1,0:T(8,128)(2,1)S(1)}, bf16[96,4096]{1,0:T(8,128)(2,1)S(1)}, u32[]{:S(2)}, u32[]{:S(2)}) collective-permute-start(bf16[96,4096]{1,0:T(8,128)(2,1)S(1)} %collective-permute-done.4), channel_id=1, source_target_pairs={{0,3},{1,0},{2,1},{3,2},{4,7},{5,4},{6,5},{7,6},{8,11},{9,8},{10,9... | collective-permute-start | bytes 2359304 | tf_op jit(solution)/shard_map/ppermute | solution.py:200
  77.3 3.0 %copy-start.27 = (f32[96,128]{1,0:T(8,128)}, f32[96,128]{1,0:T(8,128)S(1)}, u32[]{:S(2)}) copy-start(f32[96,128]{1,0:T(8,128)S(1)} %get-tuple-element.180) | copy-start | bytes 147460
  78.5 28.9 %collective-permute-start.5 = (f32[96,1280]{1,0:T(8,128)}, f32[96,1280]{1,0:T(8,128)}, u32[]{:S(2)}, u32[]{:S(2)}) collective-permute-start(f32[96,1280]{1,0:T(8,128)} %broadcast_select_fusion.2), channel_id=1, source_target_pairs={{0,8},{4,12},{8,0},{12,4},{1,9},{5,13},{9,1},{13,5},{2,10},{6,14},... | collective-permute-start | bytes 1474568 | tf_op jit(solution)/shard_map/ppermute | solution.py:136
  80.2 2.1 copy-start.22
  80.2 2.2 copy-start.24
  80.2 2.2 copy-start.30
  80.2 2.2 copy-start.33
  80.3 2.2 copy-start.36
  80.3 2.2 copy-start.39
  81.6 25.7 %collective-permute-start.6 = (f32[96,2560]{1,0:T(8,128)}, f32[96,2560]{1,0:T(8,128)}, u32[]{:S(2)}, u32[]{:S(2)}) collective-permute-start(f32[96,2560]{1,0:T(8,128)} %pad_maximum_fusion.2), channel_id=1, source_target_pairs={{0,4},{4,0},{8,12},{12,8},{1,5},{5,1},{9,13},{13,9},{2,6},{6,2},{1... | collective-permute-start | bytes 2949128 | tf_op jit(solution)/shard_map/ppermute | solution.py:136
  107.8 4.1 %copy-start.7 = (f32[96,1024]{1,0:T(8,128)S(1)}, f32[96,1024]{1,0:T(8,128)}, u32[]{:S(2)}) copy-start(f32[96,1024]{1,0:T(8,128)} %copy-done.6) | copy-start | bytes 1179652
  107.8 4.1 %copy-start.26 = (f32[96,2560]{1,0:T(8,128)S(1)}, f32[96,2560]{1,0:T(8,128)}, u32[]{:S(2)}) copy-start(f32[96,2560]{1,0:T(8,128)} %copy-done.25) | copy-start | bytes 2949124
  107.8 5.4 %collective-permute-start.9 = (f32[96,2560]{1,0:T(8,128)S(1)}, f32[96,2560]{1,0:T(8,128)S(1)}, u32[]{:S(2)}, u32[]{:S(2)}) collective-permute-start(f32[96,2560]{1,0:T(8,128)S(1)} %pad_maximum_fusion.3), channel_id=1, source_target_pairs={{0,4},{4,0},{8,12},{12,8},{1,5},{5,1},{9,13},{13,9},{2,6},{6,2},{1... | collective-permute-start | bytes 2949128 | tf_op jit(solution)/shard_map/ppermute | solution.py:136
  110.3 14.2 %collective-permute-start.8 = (f32[96,1280]{1,0:T(8,128)S(1)}, f32[96,1280]{1,0:T(8,128)S(1)}, u32[]{:S(2)}, u32[]{:S(2)}) collective-permute-start(f32[96,1280]{1,0:T(8,128)S(1)} %broadcast_select_fusion.1), channel_id=1, source_target_pairs={{0,8},{4,12},{8,0},{12,4},{1,9},{5,13},{9,1},{13,5},{2,10},{6,14},... | collective-permute-start | bytes 1474568 | tf_op jit(solution)/shard_map/ppermute | solution.py:136
  113.5 20.1 %collective-permute-start.10 = (f32[96,1280]{1,0:T(8,128)S(1)}, f32[96,1280]{1,0:T(8,128)S(1)}, u32[]{:S(2)}, u32[]{:S(2)}) collective-permute-start(f32[96,1280]{1,0:T(8,128)S(1)} %broadcast_select_fusion), channel_id=1, source_target_pairs={{0,8},{4,12},{8,0},{12,4},{1,9},{5,13},{9,1},{13,5},{2,10},{6,14},... | collective-permute-start | bytes 1474568 | tf_op jit(solution)/shard_map/ppermute | solution.py:136
  126.0 7.8 %copy-start.2 = (s32[32]{0:T(128)S(1)}, s32[32]{0:T(128)}, u32[]{:S(2)}) copy-start(s32[32]{0:T(128)} %vert_live_ref.1) | copy-start | bytes 388
  126.1 7.8 %copy-start.3 = (s32[32]{0:T(128)S(1)}, s32[32]{0:T(128)}, u32[]{:S(2)}) copy-start(s32[32]{0:T(128)} %slash_live_ref.1) | copy-start | bytes 388
  145.5 7.9 %collective-permute-start.15 = (bf16[96,1024]{1,0:T(8,128)(2,1)S(1)}, bf16[96,1024]{1,0:T(8,128)(2,1)S(1)}, u32[]{:S(2)}, u32[]{:S(2)}) collective-permute-start(bf16[96,1024]{1,0:T(8,128)(2,1)S(1)} %get-tuple-element.121), channel_id=1, source_target_pairs={{0,8},{4,12},{8,0},{12,4},{1,9},{5,13},{9,1},{13,5},{2,10},{6,14},... | collective-permute-start | bytes 589832 | tf_op jit(solution)/shard_map/ppermute | solution.py:136
  147.1 81.3 %collective-permute-start.11 = (bf16[96,1024]{1,0:T(8,128)(2,1)S(1)}, bf16[96,1024]{1,0:T(8,128)(2,1)S(1)}, u32[]{:S(2)}, u32[]{:S(2)}) collective-permute-start(bf16[96,1024]{1,0:T(8,128)(2,1)S(1)} %get-tuple-element.124), channel_id=1, source_target_pairs={{0,8},{4,12},{8,0},{12,4},{1,9},{5,13},{9,1},{13,5},{2,10},{6,14},... | collective-permute-start | bytes 589832 | tf_op jit(solution)/shard_map/ppermute | solution.py:136
  147.6 52.5 %collective-permute-start.12 = (bf16[96,1024]{1,0:T(8,128)(2,1)S(1)}, bf16[96,1024]{1,0:T(8,128)(2,1)S(1)}, u32[]{:S(2)}, u32[]{:S(2)}) collective-permute-start(bf16[96,1024]{1,0:T(8,128)(2,1)S(1)} %get-tuple-element.123), channel_id=1, source_target_pairs={{0,8},{4,12},{8,0},{12,4},{1,9},{5,13},{9,1},{13,5},{2,10},{6,14},... | collective-permute-start | bytes 589832 | tf_op jit(solution)/shard_map/ppermute | solution.py:136
  149.1 14.5 %collective-permute-start.13 = (bf16[96,1024]{1,0:T(8,128)(2,1)S(1)}, bf16[96,1024]{1,0:T(8,128)(2,1)S(1)}, u32[]{:S(2)}, u32[]{:S(2)}) collective-permute-start(bf16[96,1024]{1,0:T(8,128)(2,1)S(1)} %get-tuple-element.122), channel_id=1, source_target_pairs={{0,8},{4,12},{8,0},{12,4},{1,9},{5,13},{9,1},{13,5},{2,10},{6,14},... | collective-permute-start | bytes 589832 | tf_op jit(solution)/shard_map/ppermute | solution.py:136
  153.4 10.3 %collective-permute-start.16 = (bf16[96,2048]{1,0:T(8,128)(2,1)S(1)}, bf16[96,2048]{1,0:T(8,128)(2,1)S(1)}, u32[]{:S(2)}, u32[]{:S(2)}) collective-permute-start(bf16[96,2048]{1,0:T(8,128)(2,1)S(1)} %pad_maximum_fusion.42), channel_id=1, source_target_pairs={{0,4},{4,0},{8,12},{12,8},{1,5},{5,1},{9,13},{13,9},{2,6},{6,2},{1... | collective-permute-start | bytes 1179656 | tf_op jit(solution)/shard_map/ppermute | solution.py:136
  163.7 15.1 %collective-permute-start.14 = (bf16[96,2048]{1,0:T(8,128)(2,1)S(1)}, bf16[96,2048]{1,0:T(8,128)(2,1)S(1)}, u32[]{:S(2)}, u32[]{:S(2)}) collective-permute-start(bf16[96,2048]{1,0:T(8,128)(2,1)S(1)} %pad_maximum_fusion.41), channel_id=1, source_target_pairs={{0,4},{4,0},{8,12},{12,8},{1,5},{5,1},{9,13},{13,9},{2,6},{6,2},{1... | collective-permute-start | bytes 1179656 | tf_op jit(solution)/shard_map/ppermute | solution.py:136
  178.6 14.2 %collective-permute-start.17 = (bf16[96,2048]{1,0:T(8,128)(2,1)S(1)}, bf16[96,2048]{1,0:T(8,128)(2,1)S(1)}, u32[]{:S(2)}, u32[]{:S(2)}) collective-permute-start(bf16[96,2048]{1,0:T(8,128)(2,1)S(1)} %fusion.16), channel_id=1, source_target_pairs={{0,1},{1,2},{2,3},{3,0},{4,5},{5,6},{6,7},{7,4},{8,9},{9,10},{10,1... | collective-permute-start | bytes 1179656 | tf_op jit(solution)/shard_map/ppermute | solution.py:280
  178.8 22.2 %collective-permute-start.19 = (bf16[96,2048]{1,0:T(8,128)(2,1)S(1)}, bf16[96,2048]{1,0:T(8,128)(2,1)S(1)}, u32[]{:S(2)}, u32[]{:S(2)}) collective-permute-start(bf16[96,2048]{1,0:T(8,128)(2,1)S(1)} %fusion.19), channel_id=1, source_target_pairs={{0,1},{1,2},{2,3},{3,0},{4,5},{5,6},{6,7},{7,4},{8,9},{9,10},{10,1... | collective-permute-start | bytes 1179656 | tf_op jit(solution)/shard_map/ppermute | solution.py:280
  200.2 8.3 %collective-permute-start.18 = (bf16[96,2048]{1,0:T(8,128)(2,1)S(1)}, bf16[96,2048]{1,0:T(8,128)(2,1)S(1)}, u32[]{:S(2)}, u32[]{:S(2)}) collective-permute-start(bf16[96,2048]{1,0:T(8,128)(2,1)S(1)} %pad_maximum_fusion.43), channel_id=1, source_target_pairs={{0,4},{4,0},{8,12},{12,8},{1,5},{5,1},{9,13},{13,9},{2,6},{6,2},{1... | collective-permute-start | bytes 1179656 | tf_op jit(solution)/shard_map/ppermute | solution.py:136
  208.3 12.8 %collective-permute-start.20 = (bf16[96,2048]{1,0:T(8,128)(2,1)S(1)}, bf16[96,2048]{1,0:T(8,128)(2,1)S(1)}, u32[]{:S(2)}, u32[]{:S(2)}) collective-permute-start(bf16[96,2048]{1,0:T(8,128)(2,1)S(1)} %add_convert_fusion.5), channel_id=1, source_target_pairs={{0,1},{1,2},{2,3},{3,0},{4,5},{5,6},{6,7},{7,4},{8,9},{9,10},{10,1... | collective-permute-start | bytes 1179656 | tf_op jit(solution)/shard_map/ppermute | solution.py:280
  228.4 21.2 %collective-permute-start.21 = (bf16[96,2048]{1,0:T(8,128)(2,1)S(1)}, bf16[96,2048]{1,0:T(8,128)(2,1)S(1)}, u32[]{:S(2)}, u32[]{:S(2)}) collective-permute-start(bf16[96,2048]{1,0:T(8,128)(2,1)S(1)} %pad_maximum_fusion.44), channel_id=1, source_target_pairs={{0,4},{4,0},{8,12},{12,8},{1,5},{5,1},{9,13},{13,9},{2,6},{6,2},{1... | collective-permute-start | bytes 1179656 | tf_op jit(solution)/shard_map/ppermute | solution.py:136
  228.5 13.8 %collective-permute-start.22 = (bf16[96,2048]{1,0:T(8,128)(2,1)S(1)}, bf16[96,2048]{1,0:T(8,128)(2,1)S(1)}, u32[]{:S(2)}, u32[]{:S(2)}) collective-permute-start(bf16[96,2048]{1,0:T(8,128)(2,1)S(1)} %add_convert_fusion.4), channel_id=1, source_target_pairs={{0,1},{1,2},{2,3},{3,0},{4,5},{5,6},{6,7},{7,4},{8,9},{9,10},{10,1... | collective-permute-start | bytes 1179656 | tf_op jit(solution)/shard_map/ppermute | solution.py:280
  228.6 21.6 %collective-permute-start.23 = (bf16[96,2048]{1,0:T(8,128)(2,1)S(1)}, bf16[96,2048]{1,0:T(8,128)(2,1)S(1)}, u32[]{:S(2)}, u32[]{:S(2)}) collective-permute-start(bf16[96,2048]{1,0:T(8,128)(2,1)S(1)} %add_convert_fusion.3), channel_id=1, source_target_pairs={{0,1},{1,2},{2,3},{3,0},{4,5},{5,6},{6,7},{7,4},{8,9},{9,10},{10,1... | collective-permute-start | bytes 1179656 | tf_op jit(solution)/shard_map/ppermute | solution.py:280
  257.5 12.5 %collective-permute-start.24 = (bf16[96,2048]{1,0:T(8,128)(2,1)S(1)}, bf16[96,2048]{1,0:T(8,128)(2,1)S(1)}, u32[]{:S(2)}, u32[]{:S(2)}) collective-permute-start(bf16[96,2048]{1,0:T(8,128)(2,1)S(1)} %add_convert_fusion.2), channel_id=1, source_target_pairs={{0,1},{1,2},{2,3},{3,0},{4,5},{5,6},{6,7},{7,4},{8,9},{9,10},{10,1... | collective-permute-start | bytes 1179656 | tf_op jit(solution)/shard_map/ppermute | solution.py:280
  270.0 8.5 %copy-start.1 = (bf16[4096,256]{1,0:T(8,128)(2,1)S(1)}, bf16[4096,256]{1,0:T(8,128)(2,1)}, u32[]{:S(2)}) copy-start(bf16[4096,256]{1,0:T(8,128)(2,1)} %param.11) | copy-start | bytes 6291460
  (19 other events, 28.3 us)
